TPU v7x, 32 devices: a whole 2x2x4 slice. The times are simulated.
32 devices in a mesh: lat: 2 (over x), lon: 16 (over z, y, core).
Axes of the slice: x: 2, y: 2, z: 4, core: 2. Of those that a mesh axis runs over, the one named last changes fastest.
Arguments:
- field_state: bfloat16 [4, 16, 40960], P(None, 'lat', 'lon'), may hold values from -6 to 6
- reservoir_state: bfloat16 [4, 256, 4, 1024], P('lat', 'lon'), may hold values from -0.8984375 to 0.8984375
- coupling_blocks: bfloat16 [4, 2048, 128], P('lat'), may hold values from -0.375 to 0.375
- coupling_index: int32 [4, 8, 2], P('lat'), may hold values from 0 to 7, as said below
- input_blocks: bfloat16 [4, 1024, 128], P('lat'), may hold values from -0.5 to 0.5
- input_index: int32 [4, 8], P('lat'), may hold values from 0 to 19
- zonal_band_output_matrices: bfloat16 [2, 640, 1024], P('lat'), may hold values from -0.1875 to 0.1875
- region_band: int32 [4], P('lat'), may hold values from 0 to 1
Outputs:
- field_out: bfloat16 [4, 16, 40960], P(None, 'lat', 'lon')
- states_out: bfloat16 [4, 256, 4, 1024], P('lat', 'lon')
Inputs may be any that keep to these rules, and one draw needn't show every extreme that they name: `coupling_index`: the 2 block columns of one block-row differ. `region_band`: a band of the region row's own latitude group of 2 region rows.
All inputs are finite; a program needn't handle non-finite values.
Results may differ from a plain program's by a relative error of at most 0.0095.
Values may be sent and summed in bfloat16 or wider, within the bound.
No kernel may reach another device: no remote copies, remote signals or barrier semaphores. Data moves between devices by JAX's collectives and lax.ppermute only.
A program may use at most 64 MiB of HBM per device.

v0:
```python
import functools

import jax
import jax.numpy as jnp
from jax import lax
from jax.experimental import pallas as pl
from jax.experimental.pallas import tpu as pltpu
from jax.sharding import PartitionSpec as P

VARS = 40
STEPS = 3
CELL = 4 * VARS
CHUNK = 4 * CELL
HALF = 512
NEAR = 256
MEM = 4
BLK = 128
AHEAD = 10**10
PAD = 128
BF = jnp.bfloat16
F32 = jnp.float32
VM = pl.BlockSpec(memory_space=pltpu.VMEM)
SM = pl.BlockSpec(memory_space=pltpu.SMEM)
HB = pl.BlockSpec(memory_space=pltpu.HBM)
NT = (((1,), (1,)), ((), ()))


def row_of(slot, row_ref):
    return row_ref[0] if slot == 0 else 1 - row_ref[0]


def message_kernel(slots, row_ref, field_hbm, state_hbm, right_ref, left_ref, own_ref, *rest):
    field_ref, state_ref, sems = rest[3 * slots :]
    regions = state_hbm.shape[1]
    copies = [
        pltpu.make_async_copy(field_hbm, field_ref, sems.at[0]),
        pltpu.make_async_copy(state_hbm.at[:, pl.ds(regions - 2, 2)], state_ref.at[0], sems.at[1]),
        pltpu.make_async_copy(state_hbm.at[:, pl.ds(0, 2)], state_ref.at[1], sems.at[2]),
    ]
    for c in copies:
        c.start()
    chunks = field_ref.shape[2] // CHUNK
    copies[0].wait()
    tiles = []
    for q in range(chunks):
        for m in range(MEM):
            tiles.append(field_ref[m, :, q * CHUNK : (q + 1) * CHUNK].astype(F32)[None])
    rows = jnp.transpose(jnp.concatenate(tiles, axis=0), (1, 0, 2)).astype(BF)
    own_ref[...] = rows
    last = (chunks - 1) * MEM
    for c in copies[1:]:
        c.wait()
    for k, out in enumerate((right_ref, left_ref)):
        for r in range(2):
            for j in range(2):
                out[r, j * MEM : (j + 1) * MEM, : 2 * HALF] = state_ref[k, r, j]
        for d in range(8):
            at, lane = (d % 2) * MEM, (d // 2 % 2) * HALF
            out[2 + d // 4, at : at + MEM, lane : lane + HALF] = rows[d, last:, CHUNK - HALF :] if k == 0 else rows[d, :MEM, :HALF]
    for slot in range(slots):
        low = row_of(slot, row_ref) == 0
        dright_ref, edge_ref, dleft_ref = rest[3 * slot : 3 * slot + 3]
        for k in range(2):
            row = jnp.where(low, rows[k], rows[6 + k])
            edge_ref[k, :, :CHUNK] = row
            dright_ref[0, k * MEM : (k + 1) * MEM, :HALF] = row[last:, CHUNK - HALF :]
            dleft_ref[k * MEM : (k + 1) * MEM] = row[:MEM, :HALF]


def own_kernel(row_ref, state_ref, s0_ref, s1_ref):
    chunks = state_ref.shape[1] // 4
    for slot, s_ref in enumerate((s0_ref, s1_ref)):
        r = row_of(slot, row_ref)
        rows = [state_ref[r, 4 * q + res].astype(F32) for res in range(4) for q in range(chunks)]
        s_ref[...] = jnp.concatenate(rows, axis=0).astype(BF)


def pack(row, out_ref, k):
    last = row.shape[0] - MEM
    out_ref[k, :, :CHUNK] = row[MEM:last].astype(BF)
    half = NEAR // 2
    ends = [row[:MEM, CHUNK - NEAR : CHUNK - half], row[:MEM, CHUNK - half :], row[last:, :half], row[last:, half:NEAR]]
    out_ref[k, :, CHUNK:] = jnp.concatenate(ends, axis=0).astype(BF)


def unpack(msg):
    x = msg.astype(F32)
    own, ends = x[:, :CHUNK], x[:, CHUNK:]
    fill = jnp.zeros((MEM, CHUNK - 2 * ends.shape[1]), F32)
    before = jnp.concatenate([fill, ends[:MEM], ends[MEM : 2 * MEM]], axis=1)
    after = jnp.concatenate([ends[2 * MEM : 3 * MEM], ends[3 * MEM :], fill], axis=1)
    return jnp.concatenate([before, own, after], axis=0)


def windows(lats, narrow):
    parts = [[] for _ in range(4)]
    side = 2 * VARS
    for a in lats:
        rows = a.shape[0]
        before = jnp.concatenate([a[rows - MEM :, CHUNK - side :], a[: rows - MEM, CHUNK - side :]], axis=0)
        after = jnp.concatenate([a[MEM:, :side], a[:MEM, :side]], axis=0)
        parts[0] += [before, a[:, : 3 * side]]
        parts[1].append(a[:, side : 5 * side])
        parts[2].append(a[:, 3 * side : 7 * side])
        parts[3] += [a[:, 5 * side :], after]
    if narrow:
        parts = [[x[MEM : x.shape[0] - MEM] for x in p] for p in parts]
    return jnp.concatenate([jnp.concatenate(p, axis=1) for p in parts], axis=0).astype(BF)


def latitude(pred, d):
    per = pred.shape[0] // 4
    return jnp.concatenate([pred[res * per : (res + 1) * per, d * CELL : (d + 1) * CELL] for res in range(4)], axis=1)


def of_band(band, values, *at):
    got = values[(0, *at)]
    for g in range(1, values.shape[0]):
        got = jnp.where(band == g, values[(g, *at)], got)
    return got


def block_at(index, ref):
    return pl.multiple_of(jnp.clip(index, 0, ref.shape[1] // BLK - 1) * BLK, BLK)


def block_pre(b, band, s_ref, in_ref, cidx, iidx, coup_ref, inp_ref):
    pieces = []
    mats = [coup_ref[band, (2 * b + k) * BLK : (2 * b + k + 1) * BLK, :] for k in range(2)]
    mats.append(inp_ref[band, b * BLK : (b + 1) * BLK, :])
    for k in range(2):
        pieces.append(s_ref[:, pl.ds(block_at(of_band(band, cidx, k, b), s_ref), BLK)])
    pieces.append(in_ref[:, pl.ds(block_at(of_band(band, iidx, b), in_ref), BLK)])
    return lax.dot_general(jnp.concatenate(pieces, axis=1), jnp.concatenate(mats, axis=1), NT, preferred_element_type=F32)


def half_of(r, rest_lats):
    return pl.ds(pl.multiple_of((1 - r if rest_lats else r) * 2 * CELL, 2 * CELL), 2 * CELL)


def send_edge(r, state, read_ref, msg_ref, edge_ref, s_ref):
    s_ref[...] = state
    pred = lax.dot_general(state, read_ref[half_of(r, False), :], NT, preferred_element_type=F32)
    for d in range(2):
        row = latitude(pred, d)
        pack(row, msg_ref, d)
        edge_ref[d] = row.astype(BF)


def first_kernel(slot, edge, behind, row_ref, band_ref, cidx_ref, iidx_ref, coup_ref, inp_ref, read_ref, own_ref, s0_ref, fl_ref, *rest):
    rest = list(rest)
    r = row_of(slot, row_ref)
    if edge:
        dl_ref, lat_ref, fr_ref, dr_ref = rest[:4]
        del rest[: 4 + behind]
    else:
        fr_ref = rest[1]
        del rest[:2]
    outs, (xs_ref, s_ref, in_ref) = rest[:-3], rest[-3:]
    fill = jnp.zeros((MEM, CHUNK - HALF), F32)

    def widen(own, left, right):
        left = jnp.concatenate([fill, left.astype(F32)], axis=1)
        right = jnp.concatenate([right.astype(F32), fill], axis=1)
        return jnp.concatenate([left, own.astype(F32), right], axis=0)

    for d in range(8):
        at, lane = (d % 2) * MEM, (d // 2 % 2) * HALF
        left = fl_ref[2 + d // 4, at : at + MEM, lane : lane + HALF]
        right = fr_ref[2 + d // 4, at : at + MEM, lane : lane + HALF]
        xs_ref[2 + d] = widen(own_ref[d], left, right)
    for k in range(2):
        at = k * MEM
        if edge:
            xs_ref[10 * r + k] = widen(lat_ref[k, :, :CHUNK], dl_ref[0, at : at + MEM, :HALF], dr_ref[at : at + MEM])
        else:
            xs_ref[10 * r + k] = jnp.zeros(xs_ref.shape[1:], F32)
    empty = jnp.zeros((MEM, s0_ref.shape[1]), F32)
    per = s0_ref.shape[0] // 4
    rows = []
    for res in range(4):
        rows.append(fl_ref[r, (res - 2) * MEM : (res - 1) * MEM, : 2 * HALF].astype(F32) if res >= 2 else empty)
        rows.append(s0_ref[res * per : (res + 1) * per].astype(F32))
        rows.append(fr_ref[r, res * MEM : (res + 1) * MEM].astype(F32) if res < 2 else empty)
    s_ref[...] = jnp.concatenate(rows, axis=0).astype(BF)
    in_ref[...] = windows([xs_ref[4 * r + d] for d in range(8)], False)
    bands, cidx, iidx = band_ref[...], cidx_ref[...], iidx_ref[...]
    band = jnp.where(r == 0, bands[0], bands[1])
    pres = [block_pre(b, band, s_ref, in_ref, cidx, iidx, coup_ref, inp_ref) for b in range(iidx_ref.shape[1])]
    state = jnp.concatenate([jnp.tanh(p).astype(BF) for p in pres], axis=1)
    if edge:
        send_edge(r, state, read_ref, *outs)
        return
    outs[1][...] = state
    pred = lax.dot_general(state, read_ref[...], NT, preferred_element_type=F32)
    for d in range(4):
        outs[0][d] = latitude(pred, d).astype(BF)


def narrowed(s):
    per = s.shape[0] // 4
    return jnp.concatenate([s[res * per + MEM : (res + 1) * per - MEM] for res in range(4)], axis=0)


def shadow_kernel(last, slots, row_ref, band_ref, cidx_ref, iidx_ref, coup_ref, inp_ref, read_ref, *rest):
    rest = list(rest)

    def take(n):
        got = rest[:n]
        del rest[:n]
        return got

    edge_refs, s_refs = take(slots), take(slots)
    far_refs = take(2 * (2 - slots))
    pre_refs = take(slots)
    out_far = take(2 * (2 - slots))
    xs_ref, in_ref = take(2)
    rows_at = [row_of(0, row_ref), row_of(1, row_ref)]
    for k in range(2):
        xs_ref[k] = jnp.zeros(xs_ref.shape[1:], F32)
        xs_ref[10 + k] = jnp.zeros(xs_ref.shape[1:], F32)
    for slot in range(slots):
        r = rows_at[slot]
        pred = lax.dot_general(s_refs[slot][...], read_ref[half_of(r, True), :], NT, preferred_element_type=F32)
        for d in range(2):
            xs_ref[2 + 4 * r + 2 * r + d] = edge_refs[slot][d].astype(F32)
            xs_ref[2 + 4 * r + 2 * (1 - r) + d] = latitude(pred, d).astype(BF).astype(F32)
    if far_refs:
        for d in range(4):
            xs_ref[2 + 4 * rows_at[1] + d] = far_refs[0][d].astype(F32)
        s_refs = [s_refs[0], far_refs[1]]
    if last:
        short_refs = take(2)
        for slot in range(2):
            short_refs[slot][...] = narrowed(s_refs[slot][...].astype(F32)).astype(BF)
        s_refs = short_refs

    bands, cidx, iidx = band_ref[...], cidx_ref[...], iidx_ref[...]
    copy = None
    for slot in (1, 0):
        r = rows_at[slot]
        band = jnp.where(r == 0, bands[0], bands[1])
        in_ref[...] = windows([xs_ref[4 * r + d] for d in range(8)], last)
        blocks = iidx_ref.shape[1]
        pres = [block_pre(b, band, s_refs[slot], in_ref, cidx, iidx, coup_ref, inp_ref) for b in range(blocks)]
        if slot < slots:
            for b in range(blocks):
                pre_refs[slot][:, b * BLK : (b + 1) * BLK] = pres[b]
            continue
        state = jnp.concatenate([jnp.tanh(p).astype(BF) for p in pres], axis=1)
        if last:
            stage_ref, sem = take(2)
            copy = put_states(r, state, stage_ref, out_far[1], sem)
        else:
            out_far[1][...] = state
        pred = lax.dot_general(state, read_ref[...], NT, preferred_element_type=F32)
        for d in range(4):
            out_far[0][d] = latitude(pred, d).astype(BF)
    if copy is not None:
        copy.wait()


def put_states(r, state, stage_ref, states_hbm, sem):
    per = state.shape[0] // 4
    for res in range(4):
        for q in range(per // MEM):
            at = res * per + q * MEM
            stage_ref[4 * q + res] = state[at : at + MEM]
    copy = pltpu.make_async_copy(stage_ref, states_hbm.at[r], sem)
    copy.start()
    return copy


def late_kernel(slot, last, final, row_ref, band_ref, iidx_ref, inp_ref, read_ref, pre_ref, got_ref, *rest):
    r = row_of(slot, row_ref)
    bands, iidx = band_ref[...], iidx_ref[...]
    band = jnp.where(r == 0, bands[0], bands[1])
    in_ref = rest[-1]
    in_ref[...] = windows([unpack(got_ref[k]) for k in range(2)], last)
    parts = []
    for b in range(iidx_ref.shape[1]):
        k = of_band(band, iidx, b) - 15 * r
        used = jnp.logical_and(k >= 0, k < 5)
        at = pl.multiple_of(jnp.where(used, k, 0) * BLK, BLK)
        term = lax.dot_general(in_ref[:, pl.ds(at, BLK)], inp_ref[band, b * BLK : (b + 1) * BLK, :], NT, preferred_element_type=F32)
        pre = pre_ref[:, b * BLK : (b + 1) * BLK] + jnp.where(used, term, 0.0)
        parts.append(jnp.tanh(pre).astype(BF))
    state = jnp.concatenate(parts, axis=1)
    if not last:
        send_edge(r, state, read_ref, *rest[:3])
        return
    if not final:
        lats_ref, states_hbm, stage_ref, sem = rest[:4]
    else:
        other_ref, _, field_hbm, states_hbm, stage_ref, sem, field_ref, field_sem = rest[:8]
    copy = put_states(r, state, stage_ref, states_hbm, sem)
    pred = lax.dot_general(state, read_ref[...], NT, preferred_element_type=F32)
    mine = [latitude(pred, d) for d in range(4)]
    if not final:
        for d in range(4):
            lats_ref[d] = mine[d].astype(BF)
        copy.wait()
        return
    other = [other_ref[d].astype(F32) for d in range(4)]
    low = r == 0
    rows = [jnp.where(low, mine[d], other[d])[None] for d in range(4)]
    rows += [jnp.where(low, other[d], mine[d])[None] for d in range(4)]
    tiles = jnp.transpose(jnp.concatenate(rows, axis=0), (1, 0, 2)).astype(BF)
    for q in range(field_ref.shape[2] // CHUNK):
        for m in range(MEM):
            field_ref[m, :, q * CHUNK : (q + 1) * CHUNK] = tiles[q * MEM + m]
    out = pltpu.make_async_copy(field_ref, field_hbm, field_sem)
    out.start()
    copy.wait()
    out.wait()


def call(kernel, out_shape, out_specs, scratch, operands, flops=0, aliases=None):
    arrays = [pltpu.with_memory_space_constraint(x, pltpu.HBM) if s is HB else x for x, s in operands]
    size = sum(x.size * x.dtype.itemsize for x, _ in operands)
    return pl.pallas_call(
        kernel,
        out_shape=out_shape,
        in_specs=[s for _, s in operands],
        out_specs=out_specs,
        scratch_shapes=scratch,
        input_output_aliases=aliases or {},
        compiler_params=pltpu.CompilerParams(vmem_limit_bytes=40 * 1024 * 1024),
        cost_estimate=pl.CostEstimate(flops=flops, bytes_accessed=size, transcendentals=0),
    )(*arrays)


def per_device(field_state, reservoir_state, coupling_blocks, coupling_index, input_blocks, input_index, readout, region_band):
    lat_count, lon_count = lax.axis_size("lat"), lax.axis_size("lon")
    lat_at = lax.axis_index("lat").astype(jnp.int32)
    region_rows, regions, members, units = reservoir_state.shape
    outs = readout.shape[1]
    assert region_rows == 2 and members == MEM and regions % 4 == 0
    chunks = regions // 4
    own_rows = chunks * MEM
    wide = own_rows + 2 * MEM
    rows = 4 * wide
    short = 4 * own_rows
    swap = lat_count == 2
    slots = 1 if swap else 2

    def bf(*dims):
        return jax.ShapeDtypeStruct(dims, BF)

    def vm(dims, dtype=BF):
        return pltpu.VMEM(dims, dtype)

    def send(x, lat_step, lon_step):
        pairs = []
        for i in range(lat_count):
            to = 1 - i if swap and lat_step else i + lat_step
            if 0 <= to < lat_count:
                for j in range(lon_count):
                    pairs.append((i * lon_count + j, to * lon_count + (j + lon_step) % lon_count))
        return lax.ppermute(x, ("lat", "lon"), pairs)

    def across(xs, lon_step=0):
        if swap:
            return [send(xs[0], 1, lon_step)]
        return [send(xs[1], 1, lon_step), send(xs[0], -1, lon_step)]

    row = ((1 - lat_at if swap else lat_at * 0).reshape(1), SM)
    small = [(region_band, VM), (coupling_index.transpose(0, 2, 1), VM), (input_index, VM)]
    band, _, iidx = small
    flops = 2 * rows * units * (3 * BLK + outs)

    mail = call(
        functools.partial(message_kernel, slots),
        [bf(4, 2 * MEM, 2 * HALF + PAD), bf(4, 2 * MEM, 2 * HALF), bf(8, own_rows, CHUNK)]
        + [bf(4, 2 * MEM, 2 * HALF + PAD), bf(2, own_rows, 4 * HALF * 2 * MEM // own_rows), bf(2 * MEM, HALF)] * slots,
        [VM] * (3 + 3 * slots),
        [vm(field_state.shape), vm((2, region_rows, 2, MEM, units)), pltpu.SemaphoreType.DMA((3,))],
        [row, (field_state, HB), (reservoir_state, HB)],
        AHEAD,
    )
    from_left = send(mail[0], 0, 1)
    from_dleft = across(mail[3::3], 1)
    from_lat = across(mail[4::3])
    from_right = send(mail[1], 0, -1)
    from_dright = across(mail[5::3], -1)
    own = (mail[2], VM)
    s0, s1 = call(own_kernel, [bf(short, units)] * 2, [VM] * 2, [], [row, (reservoir_state, VM)], flops)
    weights = [(x, VM) for x in (coupling_blocks, input_blocks, readout[0])]
    states_shape = bf(region_rows, regions, MEM, units)
    stage = [vm((regions, MEM, units)), pltpu.SemaphoreType.DMA]
    padded = vm((12, wide, CHUNK), F32)
    send_out = [bf(2, own_rows, CHUNK + NEAR // 2), bf(2, wide, CHUNK), bf(rows, units)]

    sent, edges, states, far = [None] * slots, [None] * slots, [None] * slots, []
    for slot in (1, 0):
        edge = slot < slots
        operands = [row] + small + weights + [own, ((s0, s1)[slot], VM), (from_left, VM)]
        if edge:
            operands.append((from_dleft[slot], VM))
        operands.append((from_lat[slot if edge else 0], VM))
        operands.append((from_right, VM))
        if edge:
            operands.append((from_dright[slot], VM))
            operands += [(x, VM) for x in far[1:]]
        got = call(
            functools.partial(first_kernel, slot, edge, len(far[1:])),
            send_out if edge else [bf(4, wide, CHUNK), bf(rows, units)],
            [VM] * (3 if edge else 2),
            [padded, vm((rows, units)), vm((rows, 16 * CELL))],
            operands,
            flops if edge else 0,
        )
        if edge:
            sent[slot], edges[slot], states[slot] = got
        else:
            far = list(got)

    for step in range(1, STEPS):
        last = step == STEPS - 1
        got = across(sent)
        pre_rows = short if last else rows
        out = [jax.ShapeDtypeStruct((pre_rows, units), F32)] * slots
        specs = [VM] * slots
        scratch = [padded, vm((pre_rows, 16 * CELL))] + [vm((short, units))] * (2 if last else 0)
        if swap:
            out += [bf(4, own_rows if last else wide, CHUNK), states_shape if last else bf(rows, units)]
            specs += [VM, HB if last else VM]
            scratch += stage if last else []
        shadow = call(
            functools.partial(shadow_kernel, last, slots),
            out,
            specs,
            scratch,
            [row] + small + weights + [(x, VM) for x in edges + states + far],
            2 * flops,
        )
        far = list(shadow[slots:])
        for slot in reversed(range(slots)):
            operands = [row, band, iidx] + weights[1:] + [(shadow[slot], VM), (got[slot], VM)]
            inputs = [vm((pre_rows, 4 * CELL))]
            if not last:
                sent[slot], edges[slot], states[slot] = call(
                    functools.partial(late_kernel, slot, False, False), send_out, [VM] * 3, inputs, operands, flops
                )
            elif slot == 1:
                far = call(
                    functools.partial(late_kernel, slot, True, False),
                    [bf(4, own_rows, CHUNK), states_shape],
                    [VM, HB],
                    stage + inputs,
                    operands,
                    flops,
                )
            else:
                return call(
                    functools.partial(late_kernel, slot, True, True),
                    [bf(MEM, 8, regions * CELL), states_shape],
                    [HB, HB],
                    stage + [vm((MEM, 8, regions * CELL)), pltpu.SemaphoreType.DMA] + inputs,
                    operands + [(far[0], VM), (far[1], HB)],
                    flops,
                    {len(operands) + 1: 1},
                )


def solution(mesh):
    return jax.shard_map(
        per_device,
        mesh=mesh,
        in_specs=(
            P(None, "lat", "lon"),
            P("lat", "lon", None, None),
            P("lat", None, None),
            P("lat", None, None),
            P("lat", None, None),
            P("lat", None),
            P("lat", None, None),
            P("lat"),
        ),
        out_specs=(P(None, "lat", "lon"), P("lat", "lon", None, None)),
        check_vma=False,
    )
```

profile of v0, /device:TPU:0, one launch (start us, length us, event | category | flops | bytes accessed | tf_op | source)
XLA Modules:
  0.0 24.2 jit_solution(15868227467138510341)
XLA Ops:
  0.6 0.0 copy-start.6
  0.6 0.0 copy-start
  0.7 0.0 copy-start.1
  0.7 1.2 %shard_map.95 = (bf16[4,8,1152]{2,1,0:T(8,128)(2,1)S(1)}, bf16[4,8,1024]{2,1,0:T(8,128)(2,1)S(1)}, bf16[8,16,640]{2,1,0:T(8,128)(2,1)S(1)}, bf16[4,8,1152]{2,1,0...) custom-call(s32[1]{0:T(128)} %bitcast.row_ref, bf16[4,8,2560]{2,1,0:T(8,128)(2,1)} %field_hbm.1, ...), custom_call_target="tpu_custom_call" | custom-call | flops 10000000000 | bytes 425988 | tf_op jit(solution)/shard_map/pallas_call | solution.py:321
  1.9 0.5 %collective-permute-start = (bf16[4,8,1152]{2,1,0:T(8,128)(2,1)S(1)}, bf16[4,8,1152]{2,1,0:T(8,128)(2,1)S(1)}, u32[]{:S(2)}, u32[]{:S(2)}) collective-permute-start(bf16[4,8,1152]{2,1,0:T(8,128)(2,1)S(1)} %get-tuple-element.26), channel_id=1, source_target_pairs={{0,1},{1,2},{2,3},{3,4},{4,5},{5,6},{6,7},{7,8},{8,9},{9,10},{10,1... | collective-permute-start | bytes 221192 | tf_op jit(solution)/shard_map/ppermute | solution.py:360
  2.4 3.7 %collective-permute-start.1 = (bf16[4,8,1152]{2,1,0:T(8,128)(2,1)S(1)}, bf16[4,8,1152]{2,1,0:T(8,128)(2,1)S(1)}, u32[]{:S(2)}, u32[]{:S(2)}) collective-permute-start(bf16[4,8,1152]{2,1,0:T(8,128)(2,1)S(1)} %get-tuple-element.27), channel_id=1, source_target_pairs={{0,17},{1,18},{2,19},{3,20},{4,21},{5,22},{6,23},{7,24},{8,25},{9,... | collective-permute-start | bytes 221192 | tf_op jit(solution)/shard_map/ppermute | solution.py:360
  6.2 0.5 %collective-permute-start.2 = (bf16[2,16,1024]{2,1,0:T(8,128)(2,1)S(1)}, bf16[2,16,1024]{2,1,0:T(8,128)(2,1)S(1)}, u32[]{:S(2)}, u32[]{:S(2)}) collective-permute-start(bf16[2,16,1024]{2,1,0:T(8,128)(2,1)S(1)} %get-tuple-element.28), channel_id=1, source_target_pairs={{0,16},{1,17},{2,18},{3,19},{4,20},{5,21},{6,22},{7,23},{8,24},{9,... | collective-permute-start | bytes 196616 | tf_op jit(solution)/shard_map/ppermute | solution.py:360
  6.7 2.4 %collective-permute-start.3 = (bf16[4,8,1024]{2,1,0:T(8,128)(2,1)S(1)}, bf16[4,8,1024]{2,1,0:T(8,128)(2,1)S(1)}, u32[]{:S(2)}, u32[]{:S(2)}) collective-permute-start(bf16[4,8,1024]{2,1,0:T(8,128)(2,1)S(1)} %get-tuple-element.29), channel_id=1, source_target_pairs={{0,15},{1,0},{2,1},{3,2},{4,3},{5,4},{6,5},{7,6},{8,7},{9,8},{10,9... | collective-permute-start | bytes 196616 | tf_op jit(solution)/shard_map/ppermute | solution.py:360
  9.1 1.8 %collective-permute-start.4 = (bf16[8,512]{1,0:T(8,128)(2,1)S(1)}, bf16[8,512]{1,0:T(8,128)(2,1)S(1)}, u32[]{:S(2)}, u32[]{:S(2)}) collective-permute-start(bf16[8,512]{1,0:T(8,128)(2,1)S(1)} %get-tuple-element.30), channel_id=1, source_target_pairs={{0,31},{1,16},{2,17},{3,18},{4,19},{5,20},{6,21},{7,22},{8,23},{9,... | collective-permute-start | bytes 24584 | tf_op jit(solution)/shard_map/ppermute | solution.py:360
  10.9 0.0 copy-done.6
  10.9 0.1 shard_map.96
  11.0 0.0 collective-permute-done.2.rest_0_.rest_1_
  11.0 0.0 collective-permute-done.3.rest_1_.rest_2_
  11.0 0.0 collective-permute-done.fl_ref
  11.0 0.0 copy-done
  11.0 0.0 copy-done.1
  11.1 0.0 copy-done.2
  11.1 0.0 copy-done.3
  11.1 0.0 copy-done.4
  11.1 0.0 copy-done.5
  11.1 1.3 %shard_map.97 = (bf16[4,24,640]{2,1,0:T(8,128)(2,1)S(1)}, bf16[96,1024]{1,0:T(8,128)(2,1)S(1)}) custom-call(s32[1]{0:T(128)} %bitcast.row_ref, s32[2]{0:T(128)S(1)} %copy-done.5, s32[2,2,8]{2,1,0:T(2,128)S(1)} %bitcast.9, s32[2,8]{1,0:T(2,128)S(1)} %copy-done.3, bf16[2,2048,128]{2,1,0:T(8,128)(2,1)S(1)} %copy-done.2, bf16[2,1024,128]{2,1,0:T(8,128)(2,1)S(1)} %copy-done.1, ...), custom_call_target="tpu_custom_call" | custom-call | bytes 3383500 | tf_op jit(solution)/shard_map/pallas_call | solution.py:321
  12.4 0.0 collective-permute-done.4.rest_3_
  12.4 0.0 collective-permute-done.1.rest_0_
  12.4 1.1 %shard_map.98 = (bf16[2,16,768]{2,1,0:T(8,128)(2,1)S(1)}, bf16[2,24,640]{2,1,0:T(8,128)(2,1)S(1)}, bf16[96,1024]{1,0:T(8,128)(2,1)S(1)}) custom-call(s32[1]{0:T(128)} %bitcast.row_ref, s32[2]{0:T(128)S(1)} %copy-done.5, s32[2,2,8]{2,1,0:T(2,128)S(1)} %bitcast.10, s32[2,8]{1,0:T(2,128)S(1)} %copy-done.3, bf16[2,2048,128]{2,1,0:T(8,128)(2,1)S(1)} %copy-done.2, ...), custom_call_target="tpu_custom_call" | custom-call | flops 201326592 | bytes 3662028 | tf_op jit(solution)/shard_map/pallas_call | solution.py:321
  13.5 1.5 %collective-permute-start.5 = (bf16[2,16,768]{2,1,0:T(8,128)(2,1)S(1)}, bf16[2,16,768]{2,1,0:T(8,128)(2,1)S(1)}, u32[]{:S(2)}, u32[]{:S(2)}) collective-permute-start(bf16[2,16,768]{2,1,0:T(8,128)(2,1)S(1)} %get-tuple-element.37), channel_id=1, source_target_pairs={{0,16},{1,17},{2,18},{3,19},{4,20},{5,21},{6,22},{7,23},{8,24},{9,... | collective-permute-start | bytes 147464 | tf_op jit(solution)/shard_map/ppermute | solution.py:360
  15.0 2.0 %shard_map.99 = (f32[96,1024]{1,0:T(8,128)S(1)}, bf16[4,24,640]{2,1,0:T(8,128)(2,1)S(1)}, bf16[96,1024]{1,0:T(8,128)(2,1)S(1)}) custom-call(s32[1]{0:T(128)} %bitcast.row_ref, s32[2]{0:T(128)S(1)} %copy-done.5, s32[2,2,8]{2,1,0:T(2,128)S(1)} %bitcast.11, s32[2,8]{1,0:T(2,128)S(1)} %copy-done.3, bf16[2,2048,128]{2,1,0:T(8,128)(2,1)S(1)} %copy-done.2, ...), custom_call_target="tpu_custom_call" | custom-call | flops 402653184 | bytes 3461324 | tf_op jit(solution)/shard_map/pallas_call | solution.py:321
  17.0 0.7 %collective-permute-done.5.got_ref = bf16[2,16,768]{2,1,0:T(8,128)(2,1)S(1)} collective-permute-done((bf16[2,16,768]{2,1,0:T(8,128)(2,1)S(1)}, bf16[2,16,768]{2,1,0:T(8,128)(2,1)S(1)}, u32[]{:S(2)}, u32[]{:S(2)}) %collective-permute-start.5) | collective-permute-done | bytes 49184 | tf_op jit(solution)/shard_map/ppermute | solution.py:360
  17.6 0.7 %shard_map.100 = (bf16[2,16,768]{2,1,0:T(8,128)(2,1)S(1)}, bf16[2,24,640]{2,1,0:T(8,128)(2,1)S(1)}, bf16[96,1024]{1,0:T(8,128)(2,1)S(1)}) custom-call(s32[1]{0:T(128)} %bitcast.row_ref, s32[2]{0:T(128)S(1)} %copy-done.5, s32[2,8]{1,0:T(2,128)S(1)} %copy-done.3, bf16[2,1024,128]{2,1,0:T(8,128)(2,1)S(1)} %copy-done.1, bf16[640,1024]{1,0:T(8,128)(2,1)S(1)} %bitcast.6, ...), custom_call_target="tpu_custom_call" | custom-call | flops 201326592 | bytes 2277452 | tf_op jit(solution)/shard_map/pallas_call | solution.py:321
  18.4 1.5 %collective-permute-start.6 = (bf16[2,16,768]{2,1,0:T(8,128)(2,1)S(1)}, bf16[2,16,768]{2,1,0:T(8,128)(2,1)S(1)}, u32[]{:S(2)}, u32[]{:S(2)}) collective-permute-start(bf16[2,16,768]{2,1,0:T(8,128)(2,1)S(1)} %get-tuple-element.43), channel_id=1, source_target_pairs={{0,16},{1,17},{2,18},{3,19},{4,20},{5,21},{6,22},{7,23},{8,24},{9,... | collective-permute-start | bytes 147464 | tf_op jit(solution)/shard_map/ppermute | solution.py:360
  19.9 2.6 %shard_map.101 = (f32[64,1024]{1,0:T(8,128)S(1)}, bf16[4,16,640]{2,1,0:T(8,128)(2,1)S(1)}, bf16[2,16,4,1024]{3,2,1,0:T(4,128)(2,1)}) custom-call(s32[1]{0:T(128)} %bitcast.row_ref, s32[2]{0:T(128)S(1)} %copy-done.5, s32[2,2,8]{2,1,0:T(2,128)S(1)} %bitcast.12, s32[2,8]{1,0:T(2,128)S(1)} %copy-done.3, bf16[2,2048,128]{2,1,0:T(8,128)(2,1)S(1)} %copy-done.2, ...), custom_call_target="tpu_custom_call" | custom-call | flops 402653184 | bytes 3461324 | tf_op jit(solution)/shard_map/pallas_call | solution.py:321
  22.5 0.1 collective-permute-done.6.got_ref
  22.5 1.6 %shard_map.102 = (bf16[4,8,2560]{2,1,0:T(8,128)(2,1)}, bf16[2,16,4,1024]{3,2,1,0:T(4,128)(2,1)}) custom-call(s32[1]{0:T(128)} %bitcast.row_ref, s32[2]{0:T(128)S(1)} %copy-done.5, s32[2,8]{1,0:T(2,128)S(1)} %copy-done.3, bf16[2,1024,128]{2,1,0:T(8,128)(2,1)S(1)} %copy-done.1, bf16[640,1024]{1,0:T(8,128)(2,1)S(1)} %bitcast.8, ...), custom_call_target="tpu_custom_call", output_to_operand_aliasing={{1}: (8, {})} | custom-call | flops 201326592 | bytes 2490444 | tf_op jit(solution)/shard_map/pallas_call | solution.py:321
  (4 shorter events, 0.0 us)
Async XLA Ops:
  0.6 10.3 %copy-start.6 = (bf16[2,16,4,1024]{3,2,1,0:T(4,128)(2,1)S(1)}, bf16[2,16,4,1024]{3,2,1,0:T(4,128)(2,1)}, u32[]{:S(2)}) copy-start(bf16[2,16,4,1024]{3,2,1,0:T(4,128)(2,1)} %state_ref.1) | copy-start | bytes 786436
  0.6 10.4 %copy-start = (bf16[1,640,1024]{2,1,0:T(8,128)(2,1)S(1)}, bf16[1,640,1024]{2,1,0:T(8,128)(2,1)}, u32[]{:S(2)}) copy-start(bf16[1,640,1024]{2,1,0:T(8,128)(2,1)} %param.14) | copy-start | bytes 3932164
  0.7 10.4 %copy-start.1 = (bf16[2,1024,128]{2,1,0:T(8,128)(2,1)S(1)}, bf16[2,1024,128]{2,1,0:T(8,128)(2,1)}, u32[]{:S(2)}) copy-start(bf16[2,1024,128]{2,1,0:T(8,128)(2,1)} %inp_ref.11) | copy-start | bytes 1572868
  0.7 10.4 %copy-start.2 = (bf16[2,2048,128]{2,1,0:T(8,128)(2,1)S(1)}, bf16[2,2048,128]{2,1,0:T(8,128)(2,1)}, u32[]{:S(2)}) copy-start(bf16[2,2048,128]{2,1,0:T(8,128)(2,1)} %coup_ref.7) | copy-start | bytes 3145732
  0.7 10.4 %copy-start.3 = (s32[2,8]{1,0:T(2,128)S(1)}, s32[2,8]{1,0:T(2,128)}, u32[]{:S(2)}) copy-start(s32[2,8]{1,0:T(2,128)} %iidx_ref.11) | copy-start | bytes 196
  0.7 10.4 %copy-start.4 = (s32[2,8,2]{1,2,0:T(2,128)S(1)}, s32[2,8,2]{1,2,0:T(2,128)}, u32[]{:S(2)}) copy-start(s32[2,8,2]{1,2,0:T(2,128)} %param.11) | copy-start | bytes 388
  0.7 10.4 %copy-start.5 = (s32[2]{0:T(128)S(1)}, s32[2]{0:T(128)}, u32[]{:S(2)}) copy-start(s32[2]{0:T(128)} %band_ref.11) | copy-start | bytes 28
  1.9 9.1 %collective-permute-start = (bf16[4,8,1152]{2,1,0:T(8,128)(2,1)S(1)}, bf16[4,8,1152]{2,1,0:T(8,128)(2,1)S(1)}, u32[]{:S(2)}, u32[]{:S(2)}) collective-permute-start(bf16[4,8,1152]{2,1,0:T(8,128)(2,1)S(1)} %get-tuple-element.26), channel_id=1, source_target_pairs={{0,1},{1,2},{2,3},{3,4},{4,5},{5,6},{6,7},{7,8},{8,9},{9,10},{10,1... | collective-permute-start | bytes 221192 | tf_op jit(solution)/shard_map/ppermute | solution.py:360
  2.4 10.0 %collective-permute-start.1 = (bf16[4,8,1152]{2,1,0:T(8,128)(2,1)S(1)}, bf16[4,8,1152]{2,1,0:T(8,128)(2,1)S(1)}, u32[]{:S(2)}, u32[]{:S(2)}) collective-permute-start(bf16[4,8,1152]{2,1,0:T(8,128)(2,1)S(1)} %get-tuple-element.27), channel_id=1, source_target_pairs={{0,17},{1,18},{2,19},{3,20},{4,21},{5,22},{6,23},{7,24},{8,25},{9,... | collective-permute-start | bytes 221192 | tf_op jit(solution)/shard_map/ppermute | solution.py:360
  6.2 4.9 %collective-permute-start.2 = (bf16[2,16,1024]{2,1,0:T(8,128)(2,1)S(1)}, bf16[2,16,1024]{2,1,0:T(8,128)(2,1)S(1)}, u32[]{:S(2)}, u32[]{:S(2)}) collective-permute-start(bf16[2,16,1024]{2,1,0:T(8,128)(2,1)S(1)} %get-tuple-element.28), channel_id=1, source_target_pairs={{0,16},{1,17},{2,18},{3,19},{4,20},{5,21},{6,22},{7,23},{8,24},{9,... | collective-permute-start | bytes 196616 | tf_op jit(solution)/shard_map/ppermute | solution.py:360
  6.7 4.3 %collective-permute-start.3 = (bf16[4,8,1024]{2,1,0:T(8,128)(2,1)S(1)}, bf16[4,8,1024]{2,1,0:T(8,128)(2,1)S(1)}, u32[]{:S(2)}, u32[]{:S(2)}) collective-permute-start(bf16[4,8,1024]{2,1,0:T(8,128)(2,1)S(1)} %get-tuple-element.29), channel_id=1, source_target_pairs={{0,15},{1,0},{2,1},{3,2},{4,3},{5,4},{6,5},{7,6},{8,7},{9,8},{10,9... | collective-permute-start | bytes 196616 | tf_op jit(solution)/shard_map/ppermute | solution.py:360
  9.1 3.3 %collective-permute-start.4 = (bf16[8,512]{1,0:T(8,128)(2,1)S(1)}, bf16[8,512]{1,0:T(8,128)(2,1)S(1)}, u32[]{:S(2)}, u32[]{:S(2)}) collective-permute-start(bf16[8,512]{1,0:T(8,128)(2,1)S(1)} %get-tuple-element.30), channel_id=1, source_target_pairs={{0,31},{1,16},{2,17},{3,18},{4,19},{5,20},{6,21},{7,22},{8,23},{9,... | collective-permute-start | bytes 24584 | tf_op jit(solution)/shard_map/ppermute | solution.py:360
  13.5 4.2 %collective-permute-start.5 = (bf16[2,16,768]{2,1,0:T(8,128)(2,1)S(1)}, bf16[2,16,768]{2,1,0:T(8,128)(2,1)S(1)}, u32[]{:S(2)}, u32[]{:S(2)}) collective-permute-start(bf16[2,16,768]{2,1,0:T(8,128)(2,1)S(1)} %get-tuple-element.37), channel_id=1, source_target_pairs={{0,16},{1,17},{2,18},{3,19},{4,20},{5,21},{6,22},{7,23},{8,24},{9,... | collective-permute-start | bytes 147464 | tf_op jit(solution)/shard_map/ppermute | solution.py:360
  18.4 4.2 %collective-permute-start.6 = (bf16[2,16,768]{2,1,0:T(8,128)(2,1)S(1)}, bf16[2,16,768]{2,1,0:T(8,128)(2,1)S(1)}, u32[]{:S(2)}, u32[]{:S(2)}) collective-permute-start(bf16[2,16,768]{2,1,0:T(8,128)(2,1)S(1)} %get-tuple-element.43), channel_id=1, source_target_pairs={{0,16},{1,17},{2,18},{3,19},{4,20},{5,21},{6,22},{7,23},{8,24},{9,... | collective-permute-start | bytes 147464 | tf_op jit(solution)/shard_map/ppermute | solution.py:360
where the time goes:
time: 24.3 us; the launch traced here: 24.2 us
  starting transfers between devices  12 us (49%)
  Pallas kernels  10.5 us (43%)
  between operations  0.84 us (3%)
  waiting for transfers between devices  0.74 us (3%)
    ppermute x7, starting transfers between devices, send(): return lax.ppermute(x, ('lat', 'lon'), pairs)  12 us
    pallas_call x8, Pallas kernels, call(): pl.pallas_call(kernel, out_shape=out_shape, in_specs=[s for _, s in opera...  10.5 us
    ppermute x7, waiting for transfers between devices, send(): return lax.ppermute(x, ('lat', 'lon'), pairs)  0.74 us
  transfers between devices with their start and end apart: 7, of which 2 were waited for; matrix products, arithmetic and copies ran while one was open for 0% of the time, Pallas kernels for 24%

commit v1 on v0

--- a/solution.py
+++ b/solution.py
@@ -16,7 +16,7 @@
 MEM = 4
 BLK = 128
 AHEAD = 10**10
-PAD = 128
+ORDER = (3 * 10**8, 3 * 10**8)
 BF = jnp.bfloat16
 F32 = jnp.float32
 VM = pl.BlockSpec(memory_space=pltpu.VMEM)
@@ -62,17 +62,15 @@
         dright_ref, edge_ref, dleft_ref = rest[3 * slot : 3 * slot + 3]
         for k in range(2):
             row = jnp.where(low, rows[k], rows[6 + k])
-            edge_ref[k, :, :CHUNK] = row
-            dright_ref[0, k * MEM : (k + 1) * MEM, :HALF] = row[last:, CHUNK - HALF :]
+            edge_ref[k] = row
+            dright_ref[k * MEM : (k + 1) * MEM, :HALF] = row[last:, CHUNK - HALF :]
             dleft_ref[k * MEM : (k + 1) * MEM] = row[:MEM, :HALF]
 
 
-def own_kernel(row_ref, state_ref, s0_ref, s1_ref):
-    chunks = state_ref.shape[1] // 4
-    for slot, s_ref in enumerate((s0_ref, s1_ref)):
-        r = row_of(slot, row_ref)
-        rows = [state_ref[r, 4 * q + res].astype(F32) for res in range(4) for q in range(chunks)]
-        s_ref[...] = jnp.concatenate(rows, axis=0).astype(BF)
+def own_kernel(slot, row_ref, state_ref, *rest):
+    r = row_of(slot, row_ref)
+    rows = [state_ref[r, 4 * q + res].astype(F32) for res in range(4) for q in range(state_ref.shape[1] // 4)]
+    rest[-1][...] = jnp.concatenate(rows, axis=0).astype(BF)
 
 
 def pack(row, out_ref, k):
@@ -172,7 +170,7 @@
     for k in range(2):
         at = k * MEM
         if edge:
-            xs_ref[10 * r + k] = widen(lat_ref[k, :, :CHUNK], dl_ref[0, at : at + MEM, :HALF], dr_ref[at : at + MEM])
+            xs_ref[10 * r + k] = widen(lat_ref[k], dl_ref[at : at + MEM, :HALF], dr_ref[at : at + MEM])
         else:
             xs_ref[10 * r + k] = jnp.zeros(xs_ref.shape[1:], F32)
     empty = jnp.zeros((MEM, s0_ref.shape[1]), F32)
@@ -371,8 +369,7 @@
 
     mail = call(
         functools.partial(message_kernel, slots),
-        [bf(4, 2 * MEM, 2 * HALF + PAD), bf(4, 2 * MEM, 2 * HALF), bf(8, own_rows, CHUNK)]
-        + [bf(4, 2 * MEM, 2 * HALF + PAD), bf(2, own_rows, 4 * HALF * 2 * MEM // own_rows), bf(2 * MEM, HALF)] * slots,
+        [bf(4, 2 * MEM, 2 * HALF)] * 2 + [bf(8, own_rows, CHUNK)] + [bf(2 * MEM, 1536), bf(2, own_rows, CHUNK), bf(2 * MEM, HALF)] * slots,
         [VM] * (3 + 3 * slots),
         [vm(field_state.shape), vm((2, region_rows, 2, MEM, units)), pltpu.SemaphoreType.DMA((3,))],
         [row, (field_state, HB), (reservoir_state, HB)],
@@ -384,7 +381,13 @@
     from_right = send(mail[1], 0, -1)
     from_dright = across(mail[5::3], -1)
     own = (mail[2], VM)
-    s0, s1 = call(own_kernel, [bf(short, units)] * 2, [VM] * 2, [], [row, (reservoir_state, VM)], flops)
+    waits = [from_left] + from_dleft
+    s0s1 = []
+    for slot in range(2):
+        operands = [row, (reservoir_state, VM)] + [(x, VM) for x in waits]
+        s0s1.append(call(functools.partial(own_kernel, slot), bf(short, units), VM, [], operands, ORDER[slot]))
+        waits = from_lat + s0s1
+    s0, s1 = s0s1
     weights = [(x, VM) for x in (coupling_blocks, input_blocks, readout[0])]
     states_shape = bf(region_rows, regions, MEM, units)
     stage = [vm((regions, MEM, units)), pltpu.SemaphoreType.DMA]

time: 24.3 us -> 24.4 us (level)
  waiting for transfers between devices: 0.74 us -> 1.3 us
  starting transfers between devices: 12 us -> 11.7 us
    ppermute x7, waiting for transfers between devices: 0.74 us -> 1.3 us  [send(): return lax.ppermute(x, ('lat', 'lon'), pairs)]
    ppermute x7, starting transfers between devices: 12 us -> 11.7 us  [send(): return lax.ppermute(x, ('lat', 'lon'), pairs)]
    pallas_call x8 -> x9, Pallas kernels: 10.5 us -> 10.5 us  [call(): pl.pallas_call(kernel, out_shape=out_shape, in_specs=[s for _, s in opera...]
  transfers between devices with their start and end apart: 7 -> 7, of which waited for: 2 -> 3; matrix products, arithmetic and copies ran while one was open for 0% -> 0% of each run, Pallas kernels for 24% -> 24%
where the time goes in v1:
time: 24.4 us; the launch traced here: 24.3 us
  starting transfers between devices  11.7 us (48%)
  Pallas kernels  10.5 us (43%)
  waiting for transfers between devices  1.3 us (5%)
  between operations  0.83 us (3%)
    ppermute x7, starting transfers between devices, send(): return lax.ppermute(x, ('lat', 'lon'), pairs)  11.7 us
    pallas_call x9, Pallas kernels, call(): pl.pallas_call(kernel, out_shape=out_shape, in_specs=[s for _, s in opera...  10.5 us
    ppermute x7, waiting for transfers between devices, send(): return lax.ppermute(x, ('lat', 'lon'), pairs)  1.3 us
  transfers between devices with their start and end apart: 7, of which 3 were waited for; matrix products, arithmetic and copies ran while one was open for 0% of the time, Pallas kernels for 24%

profile of v1, /device:TPU:0, one launch (start us, length us, event | category | flops | bytes accessed | tf_op | source)
XLA Modules:
  0.0 24.3 jit_solution(9329747014897687611)
XLA Ops:
  0.6 0.0 copy-start.6
  0.6 0.0 copy-start.2
  0.7 1.2 %shard_map.95 = (bf16[4,8,1024]{2,1,0:T(8,128)(2,1)S(1)}, bf16[4,8,1024]{2,1,0:T(8,128)(2,1)S(1)}, bf16[8,16,640]{2,1,0:T(8,128)(2,1)S(1)}, bf16[8,1536]{1,0:T(8...) custom-call(s32[1]{0:T(128)} %bitcast.row_ref, bf16[4,8,2560]{2,1,0:T(8,128)(2,1)} %field_hbm.1, ...), custom_call_target="tpu_custom_call" | custom-call | flops 10000000000 | bytes 425988 | tf_op jit(solution)/shard_map/pallas_call | solution.py:319
  1.8 0.0 copy-start
  1.8 0.0 copy-start.1
  1.8 0.0 copy-start.3
  1.9 0.0 copy-start.4
  1.9 0.0 copy-start.5
  1.9 0.5 %collective-permute-start = (bf16[4,8,1024]{2,1,0:T(8,128)(2,1)S(1)}, bf16[4,8,1024]{2,1,0:T(8,128)(2,1)S(1)}, u32[]{:S(2)}, u32[]{:S(2)}) collective-permute-start(bf16[4,8,1024]{2,1,0:T(8,128)(2,1)S(1)} %get-tuple-element.23), channel_id=1, source_target_pairs={{0,1},{1,2},{2,3},{3,4},{4,5},{5,6},{6,7},{7,8},{8,9},{9,10},{10,1... | collective-permute-start | bytes 196616 | tf_op jit(solution)/shard_map/ppermute | solution.py:358
  2.4 3.7 %collective-permute-start.1 = (bf16[8,1536]{1,0:T(8,128)(2,1)S(1)}, bf16[8,1536]{1,0:T(8,128)(2,1)S(1)}, u32[]{:S(2)}, u32[]{:S(2)}) collective-permute-start(bf16[8,1536]{1,0:T(8,128)(2,1)S(1)} %get-tuple-element.24), channel_id=1, source_target_pairs={{0,17},{1,18},{2,19},{3,20},{4,21},{5,22},{6,23},{7,24},{8,25},{9,... | collective-permute-start | bytes 73736 | tf_op jit(solution)/shard_map/ppermute | solution.py:358
  6.1 0.5 %collective-permute-start.2 = (bf16[2,16,640]{2,1,0:T(8,128)(2,1)S(1)}, bf16[2,16,640]{2,1,0:T(8,128)(2,1)S(1)}, u32[]{:S(2)}, u32[]{:S(2)}) collective-permute-start(bf16[2,16,640]{2,1,0:T(8,128)(2,1)S(1)} %get-tuple-element.25), channel_id=1, source_target_pairs={{0,16},{1,17},{2,18},{3,19},{4,20},{5,21},{6,22},{7,23},{8,24},{9,... | collective-permute-start | bytes 122888 | tf_op jit(solution)/shard_map/ppermute | solution.py:358
  6.6 2.4 %collective-permute-start.3 = (bf16[4,8,1024]{2,1,0:T(8,128)(2,1)S(1)}, bf16[4,8,1024]{2,1,0:T(8,128)(2,1)S(1)}, u32[]{:S(2)}, u32[]{:S(2)}) collective-permute-start(bf16[4,8,1024]{2,1,0:T(8,128)(2,1)S(1)} %get-tuple-element.26), channel_id=1, source_target_pairs={{0,15},{1,0},{2,1},{3,2},{4,3},{5,4},{6,5},{7,6},{8,7},{9,8},{10,9... | collective-permute-start | bytes 196616 | tf_op jit(solution)/shard_map/ppermute | solution.py:358
  9.1 1.8 %collective-permute-start.4 = (bf16[8,512]{1,0:T(8,128)(2,1)S(1)}, bf16[8,512]{1,0:T(8,128)(2,1)S(1)}, u32[]{:S(2)}, u32[]{:S(2)}) collective-permute-start(bf16[8,512]{1,0:T(8,128)(2,1)S(1)} %get-tuple-element.27), channel_id=1, source_target_pairs={{0,31},{1,16},{2,17},{3,18},{4,19},{5,20},{6,21},{7,22},{8,23},{9,... | collective-permute-start | bytes 24584 | tf_op jit(solution)/shard_map/ppermute | solution.py:358
  10.9 0.2 collective-permute-done.1.rest_1_.rest_0_
  11.1 0.0 collective-permute-done.rest_0_.fl_ref
  11.1 0.0 copy-done.6
  11.1 0.0 collective-permute-done.2.rest_0_.rest_1_
  11.2 0.0 collective-permute-done.3.rest_1_.rest_2_
  11.2 0.0 copy-done.2
  11.2 0.0 copy-done
  11.2 0.0 copy-done.1
  11.2 1.3 %shard_map.98 = (bf16[4,24,640]{2,1,0:T(8,128)(2,1)S(1)}, bf16[96,1024]{1,0:T(8,128)(2,1)S(1)}) custom-call(s32[1]{0:T(128)} %bitcast.row_ref, s32[2]{0:T(128)S(1)} %copy-done.5, s32[2,2,8]{2,1,0:T(2,128)S(1)} %bitcast.9, s32[2,8]{1,0:T(2,128)S(1)} %copy-done.3, bf16[2,2048,128]{2,1,0:T(8,128)(2,1)S(1)} %copy-done.2, bf16[2,1024,128]{2,1,0:T(8,128)(2,1)S(1)} %copy-done.1, ...), custom_call_target="tpu_custom_call" | custom-call | bytes 3350732 | tf_op jit(solution)/shard_map/pallas_call | solution.py:319
  12.5 0.0 collective-permute-done.4.rest_3_
  12.5 1.1 %shard_map.99 = (bf16[2,16,768]{2,1,0:T(8,128)(2,1)S(1)}, bf16[2,24,640]{2,1,0:T(8,128)(2,1)S(1)}, bf16[96,1024]{1,0:T(8,128)(2,1)S(1)}) custom-call(s32[1]{0:T(128)} %bitcast.row_ref, s32[2]{0:T(128)S(1)} %copy-done.5, s32[2,2,8]{2,1,0:T(2,128)S(1)} %bitcast.10, s32[2,8]{1,0:T(2,128)S(1)} %copy-done.3, bf16[2,2048,128]{2,1,0:T(8,128)(2,1)S(1)} %copy-done.2, ...), custom_call_target="tpu_custom_call" | custom-call | flops 201326592 | bytes 3580108 | tf_op jit(solution)/shard_map/pallas_call | solution.py:319
  13.6 1.3 %collective-permute-start.5 = (bf16[2,16,768]{2,1,0:T(8,128)(2,1)S(1)}, bf16[2,16,768]{2,1,0:T(8,128)(2,1)S(1)}, u32[]{:S(2)}, u32[]{:S(2)}) collective-permute-start(bf16[2,16,768]{2,1,0:T(8,128)(2,1)S(1)} %get-tuple-element.33), channel_id=1, source_target_pairs={{0,16},{1,17},{2,18},{3,19},{4,20},{5,21},{6,22},{7,23},{8,24},{9,... | collective-permute-start | bytes 147464 | tf_op jit(solution)/shard_map/ppermute | solution.py:358
  15.0 2.0 %shard_map.100 = (f32[96,1024]{1,0:T(8,128)S(1)}, bf16[4,24,640]{2,1,0:T(8,128)(2,1)S(1)}, bf16[96,1024]{1,0:T(8,128)(2,1)S(1)}) custom-call(s32[1]{0:T(128)} %bitcast.row_ref, s32[2]{0:T(128)S(1)} %copy-done.5, s32[2,2,8]{2,1,0:T(2,128)S(1)} %bitcast.11, s32[2,8]{1,0:T(2,128)S(1)} %copy-done.3, bf16[2,2048,128]{2,1,0:T(8,128)(2,1)S(1)} %copy-done.2, ...), custom_call_target="tpu_custom_call" | custom-call | flops 402653184 | bytes 3461324 | tf_op jit(solution)/shard_map/pallas_call | solution.py:319
  16.9 0.9 %collective-permute-done.5.got_ref = bf16[2,16,768]{2,1,0:T(8,128)(2,1)S(1)} collective-permute-done((bf16[2,16,768]{2,1,0:T(8,128)(2,1)S(1)}, bf16[2,16,768]{2,1,0:T(8,128)(2,1)S(1)}, u32[]{:S(2)}, u32[]{:S(2)}) %collective-permute-start.5) | collective-permute-done | bytes 49184 | tf_op jit(solution)/shard_map/ppermute | solution.py:358
  17.8 0.7 %shard_map.101 = (bf16[2,16,768]{2,1,0:T(8,128)(2,1)S(1)}, bf16[2,24,640]{2,1,0:T(8,128)(2,1)S(1)}, bf16[96,1024]{1,0:T(8,128)(2,1)S(1)}) custom-call(s32[1]{0:T(128)} %bitcast.row_ref, s32[2]{0:T(128)S(1)} %copy-done.5, s32[2,8]{1,0:T(2,128)S(1)} %copy-done.3, bf16[2,1024,128]{2,1,0:T(8,128)(2,1)S(1)} %copy-done.1, bf16[640,1024]{1,0:T(8,128)(2,1)S(1)} %bitcast.6, ...), custom_call_target="tpu_custom_call" | custom-call | flops 201326592 | bytes 2277452 | tf_op jit(solution)/shard_map/pallas_call | solution.py:319
  18.5 1.3 %collective-permute-start.6 = (bf16[2,16,768]{2,1,0:T(8,128)(2,1)S(1)}, bf16[2,16,768]{2,1,0:T(8,128)(2,1)S(1)}, u32[]{:S(2)}, u32[]{:S(2)}) collective-permute-start(bf16[2,16,768]{2,1,0:T(8,128)(2,1)S(1)} %get-tuple-element.39), channel_id=1, source_target_pairs={{0,16},{1,17},{2,18},{3,19},{4,20},{5,21},{6,22},{7,23},{8,24},{9,... | collective-permute-start | bytes 147464 | tf_op jit(solution)/shard_map/ppermute | solution.py:358
  19.8 2.6 %shard_map.102 = (f32[64,1024]{1,0:T(8,128)S(1)}, bf16[4,16,640]{2,1,0:T(8,128)(2,1)S(1)}, bf16[2,16,4,1024]{3,2,1,0:T(4,128)(2,1)}) custom-call(s32[1]{0:T(128)} %bitcast.row_ref, s32[2]{0:T(128)S(1)} %copy-done.5, s32[2,2,8]{2,1,0:T(2,128)S(1)} %bitcast.12, s32[2,8]{1,0:T(2,128)S(1)} %copy-done.3, bf16[2,2048,128]{2,1,0:T(8,128)(2,1)S(1)} %copy-done.2, ...), custom_call_target="tpu_custom_call" | custom-call | flops 402653184 | bytes 3461324 | tf_op jit(solution)/shard_map/pallas_call | solution.py:319
  22.4 0.3 %collective-permute-done.6.got_ref = bf16[2,16,768]{2,1,0:T(8,128)(2,1)S(1)} collective-permute-done((bf16[2,16,768]{2,1,0:T(8,128)(2,1)S(1)}, bf16[2,16,768]{2,1,0:T(8,128)(2,1)S(1)}, u32[]{:S(2)}, u32[]{:S(2)}) %collective-permute-start.6) | collective-permute-done | bytes 49184 | tf_op jit(solution)/shard_map/ppermute | solution.py:358
  22.7 1.6 %shard_map.103 = (bf16[4,8,2560]{2,1,0:T(8,128)(2,1)}, bf16[2,16,4,1024]{3,2,1,0:T(4,128)(2,1)}) custom-call(s32[1]{0:T(128)} %bitcast.row_ref, s32[2]{0:T(128)S(1)} %copy-done.5, s32[2,8]{1,0:T(2,128)S(1)} %copy-done.3, bf16[2,1024,128]{2,1,0:T(8,128)(2,1)S(1)} %copy-done.1, bf16[640,1024]{1,0:T(8,128)(2,1)S(1)} %bitcast.8, ...), custom_call_target="tpu_custom_call", output_to_operand_aliasing={{1}: (8, {})} | custom-call | flops 201326592 | bytes 2490444 | tf_op jit(solution)/shard_map/pallas_call | solution.py:319
  (5 shorter events, 0.1 us)
Async XLA Ops:
  0.6 10.4 %copy-start.6 = (bf16[2,16,4,1024]{3,2,1,0:T(4,128)(2,1)S(1)}, bf16[2,16,4,1024]{3,2,1,0:T(4,128)(2,1)}, u32[]{:S(2)}) copy-start(bf16[2,16,4,1024]{3,2,1,0:T(4,128)(2,1)} %state_ref.3) | copy-start | bytes 786436
  0.6 10.5 %copy-start.2 = (bf16[2,2048,128]{2,1,0:T(8,128)(2,1)S(1)}, bf16[2,2048,128]{2,1,0:T(8,128)(2,1)}, u32[]{:S(2)}) copy-start(bf16[2,2048,128]{2,1,0:T(8,128)(2,1)} %coup_ref.7) | copy-start | bytes 3145732
  1.8 9.4 %copy-start = (bf16[1,640,1024]{2,1,0:T(8,128)(2,1)S(1)}, bf16[1,640,1024]{2,1,0:T(8,128)(2,1)}, u32[]{:S(2)}) copy-start(bf16[1,640,1024]{2,1,0:T(8,128)(2,1)} %param.14) | copy-start | bytes 3932164
  1.8 9.4 %copy-start.1 = (bf16[2,1024,128]{2,1,0:T(8,128)(2,1)S(1)}, bf16[2,1024,128]{2,1,0:T(8,128)(2,1)}, u32[]{:S(2)}) copy-start(bf16[2,1024,128]{2,1,0:T(8,128)(2,1)} %inp_ref.11) | copy-start | bytes 1572868
  1.8 9.4 %copy-start.3 = (s32[2,8]{1,0:T(2,128)S(1)}, s32[2,8]{1,0:T(2,128)}, u32[]{:S(2)}) copy-start(s32[2,8]{1,0:T(2,128)} %iidx_ref.11) | copy-start | bytes 196
  1.9 9.4 %copy-start.4 = (s32[2,8,2]{1,2,0:T(2,128)S(1)}, s32[2,8,2]{1,2,0:T(2,128)}, u32[]{:S(2)}) copy-start(s32[2,8,2]{1,2,0:T(2,128)} %param.11) | copy-start | bytes 388
  1.9 9.4 %copy-start.5 = (s32[2]{0:T(128)S(1)}, s32[2]{0:T(128)}, u32[]{:S(2)}) copy-start(s32[2]{0:T(128)} %band_ref.11) | copy-start | bytes 28
  1.9 9.2 %collective-permute-start = (bf16[4,8,1024]{2,1,0:T(8,128)(2,1)S(1)}, bf16[4,8,1024]{2,1,0:T(8,128)(2,1)S(1)}, u32[]{:S(2)}, u32[]{:S(2)}) collective-permute-start(bf16[4,8,1024]{2,1,0:T(8,128)(2,1)S(1)} %get-tuple-element.23), channel_id=1, source_target_pairs={{0,1},{1,2},{2,3},{3,4},{4,5},{5,6},{6,7},{7,8},{8,9},{9,10},{10,1... | collective-permute-start | bytes 196616 | tf_op jit(solution)/shard_map/ppermute | solution.py:358
  2.4 8.7 %collective-permute-start.1 = (bf16[8,1536]{1,0:T(8,128)(2,1)S(1)}, bf16[8,1536]{1,0:T(8,128)(2,1)S(1)}, u32[]{:S(2)}, u32[]{:S(2)}) collective-permute-start(bf16[8,1536]{1,0:T(8,128)(2,1)S(1)} %get-tuple-element.24), channel_id=1, source_target_pairs={{0,17},{1,18},{2,19},{3,20},{4,21},{5,22},{6,23},{7,24},{8,25},{9,... | collective-permute-start | bytes 73736 | tf_op jit(solution)/shard_map/ppermute | solution.py:358
  6.1 5.0 %collective-permute-start.2 = (bf16[2,16,640]{2,1,0:T(8,128)(2,1)S(1)}, bf16[2,16,640]{2,1,0:T(8,128)(2,1)S(1)}, u32[]{:S(2)}, u32[]{:S(2)}) collective-permute-start(bf16[2,16,640]{2,1,0:T(8,128)(2,1)S(1)} %get-tuple-element.25), channel_id=1, source_target_pairs={{0,16},{1,17},{2,18},{3,19},{4,20},{5,21},{6,22},{7,23},{8,24},{9,... | collective-permute-start | bytes 122888 | tf_op jit(solution)/shard_map/ppermute | solution.py:358
  6.6 4.5 %collective-permute-start.3 = (bf16[4,8,1024]{2,1,0:T(8,128)(2,1)S(1)}, bf16[4,8,1024]{2,1,0:T(8,128)(2,1)S(1)}, u32[]{:S(2)}, u32[]{:S(2)}) collective-permute-start(bf16[4,8,1024]{2,1,0:T(8,128)(2,1)S(1)} %get-tuple-element.26), channel_id=1, source_target_pairs={{0,15},{1,0},{2,1},{3,2},{4,3},{5,4},{6,5},{7,6},{8,7},{9,8},{10,9... | collective-permute-start | bytes 196616 | tf_op jit(solution)/shard_map/ppermute | solution.py:358
  9.1 3.5 %collective-permute-start.4 = (bf16[8,512]{1,0:T(8,128)(2,1)S(1)}, bf16[8,512]{1,0:T(8,128)(2,1)S(1)}, u32[]{:S(2)}, u32[]{:S(2)}) collective-permute-start(bf16[8,512]{1,0:T(8,128)(2,1)S(1)} %get-tuple-element.27), channel_id=1, source_target_pairs={{0,31},{1,16},{2,17},{3,18},{4,19},{5,20},{6,21},{7,22},{8,23},{9,... | collective-permute-start | bytes 24584 | tf_op jit(solution)/shard_map/ppermute | solution.py:358
  13.6 4.2 %collective-permute-start.5 = (bf16[2,16,768]{2,1,0:T(8,128)(2,1)S(1)}, bf16[2,16,768]{2,1,0:T(8,128)(2,1)S(1)}, u32[]{:S(2)}, u32[]{:S(2)}) collective-permute-start(bf16[2,16,768]{2,1,0:T(8,128)(2,1)S(1)} %get-tuple-element.33), channel_id=1, source_target_pairs={{0,16},{1,17},{2,18},{3,19},{4,20},{5,21},{6,22},{7,23},{8,24},{9,... | collective-permute-start | bytes 147464 | tf_op jit(solution)/shard_map/ppermute | solution.py:358
  18.5 4.2 %collective-permute-start.6 = (bf16[2,16,768]{2,1,0:T(8,128)(2,1)S(1)}, bf16[2,16,768]{2,1,0:T(8,128)(2,1)S(1)}, u32[]{:S(2)}, u32[]{:S(2)}) collective-permute-start(bf16[2,16,768]{2,1,0:T(8,128)(2,1)S(1)} %get-tuple-element.39), channel_id=1, source_target_pairs={{0,16},{1,17},{2,18},{3,19},{4,20},{5,21},{6,22},{7,23},{8,24},{9,... | collective-permute-start | bytes 147464 | tf_op jit(solution)/shard_map/ppermute | solution.py:358

commit v2 on v1

--- a/solution.py
+++ b/solution.py
@@ -67,10 +67,46 @@
             dleft_ref[k * MEM : (k + 1) * MEM] = row[:MEM, :HALF]
 
 
-def own_kernel(slot, row_ref, state_ref, *rest):
+def own_kernel(slot, row_ref, state_ref, band_ref, cidx_ref, iidx_ref, *rest):
+    s_ref, code_ref = rest[-2:]
     r = row_of(slot, row_ref)
     rows = [state_ref[r, 4 * q + res].astype(F32) for res in range(4) for q in range(state_ref.shape[1] // 4)]
-    rest[-1][...] = jnp.concatenate(rows, axis=0).astype(BF)
+    s_ref[...] = jnp.concatenate(rows, axis=0).astype(BF)
+    bands = band_ref[...]
+    band = jnp.where(r == 0, bands[0], bands[1])
+
+    def chosen(values):
+        got = values[0]
+        for g in range(1, values.shape[0]):
+            got = jnp.where(band == g, values[g], got)
+        return got.astype(F32)
+
+    blocks = iidx_ref.shape[1]
+    at = lax.broadcasted_iota(jnp.int32, (1, blocks), 1)
+    weights = [sum(jnp.where(at == b, 2.0 ** (3 * b), 0.0) for b in range(blocks))]
+    for half in range(2):
+        weights.append(sum(jnp.where(at == b, 2.0 ** (5 * (b % 4)), 0.0) for b in range(4 * half, 4 * half + 4)))
+    columns, inputs = chosen(cidx_ref[...]), chosen(iidx_ref[...])
+    words = [jnp.sum(columns[k : k + 1] * weights[0]) for k in range(2)]
+    words += [jnp.sum(inputs.reshape(1, blocks) * weights[1 + half]) for half in range(2)]
+    lane = lax.broadcasted_iota(jnp.int32, code_ref.shape, 1)
+    code = jnp.where(lane == 0, band.astype(F32), 0.0)
+    for k, word in enumerate(words):
+        code = jnp.where(lane == k + 1, word, code)
+    code_ref[...] = code.astype(jnp.int32)
+
+
+def decode(code_ref):
+    code = code_ref[...]
+    band, columns, inputs = code[0, 0], [code[0, 1 + k] for k in range(2)], [code[0, 3 + k] for k in range(2)]
+
+    def column(k, b):
+        return (columns[k] >> (3 * b)) & 7
+
+    def source(b):
+        return (inputs[b // 4] >> (5 * (b % 4))) & 31
+
+    return band, column, source
 
 
 def pack(row, out_ref, k):
@@ -111,24 +147,18 @@
     return jnp.concatenate([pred[res * per : (res + 1) * per, d * CELL : (d + 1) * CELL] for res in range(4)], axis=1)
 
 
-def of_band(band, values, *at):
-    got = values[(0, *at)]
-    for g in range(1, values.shape[0]):
-        got = jnp.where(band == g, values[(g, *at)], got)
-    return got
-
-
 def block_at(index, ref):
     return pl.multiple_of(jnp.clip(index, 0, ref.shape[1] // BLK - 1) * BLK, BLK)
 
 
-def block_pre(b, band, s_ref, in_ref, cidx, iidx, coup_ref, inp_ref):
+def block_pre(b, codes, s_ref, in_ref, coup_ref, inp_ref):
+    band, column, source = codes
     pieces = []
     mats = [coup_ref[band, (2 * b + k) * BLK : (2 * b + k + 1) * BLK, :] for k in range(2)]
     mats.append(inp_ref[band, b * BLK : (b + 1) * BLK, :])
     for k in range(2):
-        pieces.append(s_ref[:, pl.ds(block_at(of_band(band, cidx, k, b), s_ref), BLK)])
-    pieces.append(in_ref[:, pl.ds(block_at(of_band(band, iidx, b), in_ref), BLK)])
+        pieces.append(s_ref[:, pl.ds(block_at(column(k, b), s_ref), BLK)])
+    pieces.append(in_ref[:, pl.ds(block_at(source(b), in_ref), BLK)])
     return lax.dot_general(jnp.concatenate(pieces, axis=1), jnp.concatenate(mats, axis=1), NT, preferred_element_type=F32)
 
 
@@ -145,7 +175,7 @@
         edge_ref[d] = row.astype(BF)
 
 
-def first_kernel(slot, edge, behind, row_ref, band_ref, cidx_ref, iidx_ref, coup_ref, inp_ref, read_ref, own_ref, s0_ref, fl_ref, *rest):
+def first_kernel(slot, edge, behind, row_ref, code_ref, coup_ref, inp_ref, read_ref, own_ref, s0_ref, fl_ref, *rest):
     rest = list(rest)
     r = row_of(slot, row_ref)
     if edge:
@@ -182,9 +212,8 @@
         rows.append(fr_ref[r, res * MEM : (res + 1) * MEM].astype(F32) if res < 2 else empty)
     s_ref[...] = jnp.concatenate(rows, axis=0).astype(BF)
     in_ref[...] = windows([xs_ref[4 * r + d] for d in range(8)], False)
-    bands, cidx, iidx = band_ref[...], cidx_ref[...], iidx_ref[...]
-    band = jnp.where(r == 0, bands[0], bands[1])
-    pres = [block_pre(b, band, s_ref, in_ref, cidx, iidx, coup_ref, inp_ref) for b in range(iidx_ref.shape[1])]
+    codes = decode(code_ref)
+    pres = [block_pre(b, codes, s_ref, in_ref, coup_ref, inp_ref) for b in range(s_ref.shape[1] // BLK)]
     state = jnp.concatenate([jnp.tanh(p).astype(BF) for p in pres], axis=1)
     if edge:
         send_edge(r, state, read_ref, *outs)
@@ -200,7 +229,7 @@
     return jnp.concatenate([s[res * per + MEM : (res + 1) * per - MEM] for res in range(4)], axis=0)
 
 
-def shadow_kernel(last, slots, row_ref, band_ref, cidx_ref, iidx_ref, coup_ref, inp_ref, read_ref, *rest):
+def shadow_kernel(last, slots, row_ref, code0_ref, code1_ref, coup_ref, inp_ref, read_ref, *rest):
     rest = list(rest)
 
     def take(n):
@@ -233,14 +262,13 @@
             short_refs[slot][...] = narrowed(s_refs[slot][...].astype(F32)).astype(BF)
         s_refs = short_refs
 
-    bands, cidx, iidx = band_ref[...], cidx_ref[...], iidx_ref[...]
     copy = None
     for slot in (1, 0):
         r = rows_at[slot]
-        band = jnp.where(r == 0, bands[0], bands[1])
+        codes = decode((code0_ref, code1_ref)[slot])
         in_ref[...] = windows([xs_ref[4 * r + d] for d in range(8)], last)
-        blocks = iidx_ref.shape[1]
-        pres = [block_pre(b, band, s_refs[slot], in_ref, cidx, iidx, coup_ref, inp_ref) for b in range(blocks)]
+        blocks = s_refs[slot].shape[1] // BLK
+        pres = [block_pre(b, codes, s_refs[slot], in_ref, coup_ref, inp_ref) for b in range(blocks)]
         if slot < slots:
             for b in range(blocks):
                 pre_refs[slot][:, b * BLK : (b + 1) * BLK] = pres[b]
@@ -269,15 +297,14 @@
     return copy
 
 
-def late_kernel(slot, last, final, row_ref, band_ref, iidx_ref, inp_ref, read_ref, pre_ref, got_ref, *rest):
+def late_kernel(slot, last, final, row_ref, code_ref, inp_ref, read_ref, pre_ref, got_ref, *rest):
     r = row_of(slot, row_ref)
-    bands, iidx = band_ref[...], iidx_ref[...]
-    band = jnp.where(r == 0, bands[0], bands[1])
+    band, _, source = decode(code_ref)
     in_ref = rest[-1]
     in_ref[...] = windows([unpack(got_ref[k]) for k in range(2)], last)
     parts = []
-    for b in range(iidx_ref.shape[1]):
-        k = of_band(band, iidx, b) - 15 * r
+    for b in range(pre_ref.shape[1] // BLK):
+        k = source(b) - 15 * r
         used = jnp.logical_and(k >= 0, k < 5)
         at = pl.multiple_of(jnp.where(used, k, 0) * BLK, BLK)
         term = lax.dot_general(in_ref[:, pl.ds(at, BLK)], inp_ref[band, b * BLK : (b + 1) * BLK, :], NT, preferred_element_type=F32)
@@ -333,7 +360,7 @@
     lat_at = lax.axis_index("lat").astype(jnp.int32)
     region_rows, regions, members, units = reservoir_state.shape
     outs = readout.shape[1]
-    assert region_rows == 2 and members == MEM and regions % 4 == 0
+    assert region_rows == 2 and members == MEM and regions % 4 == 0 and units == 8 * BLK
     chunks = regions // 4
     own_rows = chunks * MEM
     wide = own_rows + 2 * MEM
@@ -364,7 +391,6 @@
 
     row = ((1 - lat_at if swap else lat_at * 0).reshape(1), SM)
     small = [(region_band, VM), (coupling_index.transpose(0, 2, 1), VM), (input_index, VM)]
-    band, _, iidx = small
     flops = 2 * rows * units * (3 * BLK + outs)
 
     mail = call(
@@ -384,10 +410,12 @@
     waits = [from_left] + from_dleft
     s0s1 = []
     for slot in range(2):
-        operands = [row, (reservoir_state, VM)] + [(x, VM) for x in waits]
-        s0s1.append(call(functools.partial(own_kernel, slot), bf(short, units), VM, [], operands, ORDER[slot]))
-        waits = from_lat + s0s1
-    s0, s1 = s0s1
+        operands = [row, (reservoir_state, VM)] + small + [(x, VM) for x in waits]
+        words = jax.ShapeDtypeStruct((8, BLK), jnp.int32)
+        s0s1.append(call(functools.partial(own_kernel, slot), [bf(short, units), words], [VM] * 2, [], operands, ORDER[slot]))
+        waits = from_lat + [s0s1[-1][0]]
+    (s0, code0), (s1, code1) = s0s1
+    codes = [(code0, VM), (code1, VM)]
     weights = [(x, VM) for x in (coupling_blocks, input_blocks, readout[0])]
     states_shape = bf(region_rows, regions, MEM, units)
     stage = [vm((regions, MEM, units)), pltpu.SemaphoreType.DMA]
@@ -397,7 +425,7 @@
     sent, edges, states, far = [None] * slots, [None] * slots, [None] * slots, []
     for slot in (1, 0):
         edge = slot < slots
-        operands = [row] + small + weights + [own, ((s0, s1)[slot], VM), (from_left, VM)]
+        operands = [row, codes[slot]] + weights + [own, ((s0, s1)[slot], VM), (from_left, VM)]
         if edge:
             operands.append((from_dleft[slot], VM))
         operands.append((from_lat[slot if edge else 0], VM))
@@ -434,12 +462,12 @@
             out,
             specs,
             scratch,
-            [row] + small + weights + [(x, VM) for x in edges + states + far],
+            [row] + codes + weights + [(x, VM) for x in edges + states + far],
             2 * flops,
         )
         far = list(shadow[slots:])
         for slot in reversed(range(slots)):
-            operands = [row, band, iidx] + weights[1:] + [(shadow[slot], VM), (got[slot], VM)]
+            operands = [row, codes[slot]] + weights[1:] + [(shadow[slot], VM), (got[slot], VM)]
             inputs = [vm((pre_rows, 4 * CELL))]
             if not last:
                 sent[slot], edges[slot], states[slot] = call(

time: 24.4 us -> 24.7 us (1.012)
  waiting for transfers between devices: 1.3 us -> 2.25 us
  starting transfers between devices: 11.7 us -> 10.8 us
    ppermute x7, waiting for transfers between devices: 1.3 us -> 2.25 us  [send(): return lax.ppermute(x, ('lat', 'lon'), pairs)]
    ppermute x7, starting transfers between devices: 11.7 us -> 10.8 us  [send(): return lax.ppermute(x, ('lat', 'lon'), pairs)]
  transfers between devices with their start and end apart: 7 -> 7, of which waited for: 3 -> 3; matrix products, arithmetic and copies ran while one was open for 0% -> 0% of each run, Pallas kernels for 24% -> 25%
where the time goes in v2:
time: 24.7 us; the launch traced here: 24.5 us
  starting transfers between devices  10.8 us (44%)
  Pallas kernels  10.6 us (43%)
  waiting for transfers between devices  2.25 us (9%)
  between operations  0.83 us (3%)
    ppermute x7, starting transfers between devices, send(): return lax.ppermute(x, ('lat', 'lon'), pairs)  10.8 us
    pallas_call x9, Pallas kernels, call(): pl.pallas_call(kernel, out_shape=out_shape, in_specs=[s for _, s in opera...  10.6 us
    ppermute x7, waiting for transfers between devices, send(): return lax.ppermute(x, ('lat', 'lon'), pairs)  2.25 us
  transfers between devices with their start and end apart: 7, of which 3 were waited for; matrix products, arithmetic and copies ran while one was open for 0% of the time, Pallas kernels for 25%

profile of v2, /device:TPU:0, one launch (start us, length us, event | category | flops | bytes accessed | tf_op | source)
XLA Modules:
  0.0 24.5 jit_solution(17812702224970232219)
XLA Ops:
  0.6 0.0 copy-start.3
  0.6 0.0 copy-start.4
  0.7 0.0 copy-start.5
  0.7 0.0 copy-start.6
  0.7 0.0 copy-start.2
  0.7 1.2 %shard_map.95 = (bf16[4,8,1024]{2,1,0:T(8,128)(2,1)S(1)}, bf16[4,8,1024]{2,1,0:T(8,128)(2,1)S(1)}, bf16[8,16,640]{2,1,0:T(8,128)(2,1)S(1)}, bf16[8,1536]{1,0:T(8...) custom-call(s32[1]{0:T(128)} %bitcast.row_ref, bf16[4,8,2560]{2,1,0:T(8,128)(2,1)} %field_hbm.1, ...), custom_call_target="tpu_custom_call" | custom-call | flops 10000000000 | bytes 425988 | tf_op jit(solution)/shard_map/pallas_call | solution.py:346
  1.8 0.0 copy-start
  1.9 0.0 copy-start.1
  1.9 0.5 %collective-permute-start = (bf16[4,8,1024]{2,1,0:T(8,128)(2,1)S(1)}, bf16[4,8,1024]{2,1,0:T(8,128)(2,1)S(1)}, u32[]{:S(2)}, u32[]{:S(2)}) collective-permute-start(bf16[4,8,1024]{2,1,0:T(8,128)(2,1)S(1)} %get-tuple-element.26), channel_id=1, source_target_pairs={{0,1},{1,2},{2,3},{3,4},{4,5},{5,6},{6,7},{7,8},{8,9},{9,10},{10,1... | collective-permute-start | bytes 196616 | tf_op jit(solution)/shard_map/ppermute | solution.py:385
  2.4 3.7 %collective-permute-start.1 = (bf16[8,1536]{1,0:T(8,128)(2,1)S(1)}, bf16[8,1536]{1,0:T(8,128)(2,1)S(1)}, u32[]{:S(2)}, u32[]{:S(2)}) collective-permute-start(bf16[8,1536]{1,0:T(8,128)(2,1)S(1)} %get-tuple-element.27), channel_id=1, source_target_pairs={{0,17},{1,18},{2,19},{3,20},{4,21},{5,22},{6,23},{7,24},{8,25},{9,... | collective-permute-start | bytes 73736 | tf_op jit(solution)/shard_map/ppermute | solution.py:385
  6.1 0.5 %collective-permute-start.2 = (bf16[2,16,640]{2,1,0:T(8,128)(2,1)S(1)}, bf16[2,16,640]{2,1,0:T(8,128)(2,1)S(1)}, u32[]{:S(2)}, u32[]{:S(2)}) collective-permute-start(bf16[2,16,640]{2,1,0:T(8,128)(2,1)S(1)} %get-tuple-element.29), channel_id=1, source_target_pairs={{0,16},{1,17},{2,18},{3,19},{4,20},{5,21},{6,22},{7,23},{8,24},{9,... | collective-permute-start | bytes 122888 | tf_op jit(solution)/shard_map/ppermute | solution.py:385
  6.6 2.4 %collective-permute-start.3 = (bf16[4,8,1024]{2,1,0:T(8,128)(2,1)S(1)}, bf16[4,8,1024]{2,1,0:T(8,128)(2,1)S(1)}, u32[]{:S(2)}, u32[]{:S(2)}) collective-permute-start(bf16[4,8,1024]{2,1,0:T(8,128)(2,1)S(1)} %get-tuple-element.33), channel_id=1, source_target_pairs={{0,15},{1,0},{2,1},{3,2},{4,3},{5,4},{6,5},{7,6},{8,7},{9,8},{10,9... | collective-permute-start | bytes 196616 | tf_op jit(solution)/shard_map/ppermute | solution.py:385
  9.1 1.8 %collective-permute-start.4 = (bf16[8,512]{1,0:T(8,128)(2,1)S(1)}, bf16[8,512]{1,0:T(8,128)(2,1)S(1)}, u32[]{:S(2)}, u32[]{:S(2)}) collective-permute-start(bf16[8,512]{1,0:T(8,128)(2,1)S(1)} %get-tuple-element.34), channel_id=1, source_target_pairs={{0,31},{1,16},{2,17},{3,18},{4,19},{5,20},{6,21},{7,22},{8,23},{9,... | collective-permute-start | bytes 24584 | tf_op jit(solution)/shard_map/ppermute | solution.py:385
  10.9 0.2 collective-permute-done.1.rest_1_.rest_0_
  11.1 0.0 collective-permute-done.rest_0_.fl_ref
  11.1 0.0 copy-done.3
  11.1 0.0 copy-done.4
  11.1 0.2 shard_map.96
  11.3 0.0 collective-permute-done.2.rest_0_.rest_1_
  11.3 0.2 shard_map.97
  11.6 0.0 collective-permute-done.3.rest_1_.rest_2_
  11.6 1.2 %shard_map.98 = (bf16[4,24,640]{2,1,0:T(8,128)(2,1)S(1)}, bf16[96,1024]{1,0:T(8,128)(2,1)S(1)}) custom-call(s32[1]{0:T(128)} %bitcast.row_ref, s32[8,128]{1,0:T(8,128)S(1)} %get-tuple-element.31.code_ref.code1_ref, bf16[2,2048,128]{2,1,0:T(8,128)(2,1)S(1)} %copy-done.2, bf16[2,1024,128]{2,1,0:T(8,128)(2,1)S(1)} %copy-done.1, bf16[640,1024]{1,0:T(8,128)(2,1)S(1)} %bitcast.3, ...), custom_call_target="tpu_custom_call" | custom-call | bytes 3354628 | tf_op jit(solution)/shard_map/pallas_call | solution.py:346
  12.8 0.0 collective-permute-done.4.rest_3_
  12.8 1.0 %shard_map.99 = (bf16[2,16,768]{2,1,0:T(8,128)(2,1)S(1)}, bf16[2,24,640]{2,1,0:T(8,128)(2,1)S(1)}, bf16[96,1024]{1,0:T(8,128)(2,1)S(1)}) custom-call(s32[1]{0:T(128)} %bitcast.row_ref, s32[8,128]{1,0:T(8,128)S(1)} %get-tuple-element.28.code_ref.code0_ref, bf16[2,2048,128]{2,1,0:T(8,128)(2,1)S(1)} %copy-done.2, bf16[2,1024,128]{2,1,0:T(8,128)(2,1)S(1)} %copy-done.1, ...), custom_call_target="tpu_custom_call" | custom-call | flops 201326592 | bytes 3584004 | tf_op jit(solution)/shard_map/pallas_call | solution.py:346
  13.9 0.9 %collective-permute-start.5 = (bf16[2,16,768]{2,1,0:T(8,128)(2,1)S(1)}, bf16[2,16,768]{2,1,0:T(8,128)(2,1)S(1)}, u32[]{:S(2)}, u32[]{:S(2)}) collective-permute-start(bf16[2,16,768]{2,1,0:T(8,128)(2,1)S(1)} %get-tuple-element.41), channel_id=1, source_target_pairs={{0,16},{1,17},{2,18},{3,19},{4,20},{5,21},{6,22},{7,23},{8,24},{9,... | collective-permute-start | bytes 147464 | tf_op jit(solution)/shard_map/ppermute | solution.py:385
  14.8 2.0 %shard_map.100 = (f32[96,1024]{1,0:T(8,128)S(1)}, bf16[4,24,640]{2,1,0:T(8,128)(2,1)S(1)}, bf16[96,1024]{1,0:T(8,128)(2,1)S(1)}) custom-call(s32[1]{0:T(128)} %bitcast.row_ref, s32[8,128]{1,0:T(8,128)S(1)} %get-tuple-element.28.code_ref.code0_ref, s32[8,128]{1,0:T(8,128)S(1)} %get-tuple-element.31.code_ref.code1_ref, bf16[2,2048,128]{2,1,0:T(8,128)(2,1)S(1)} %copy-done.2, ...), custom_call_target="tpu_custom_call" | custom-call | flops 402653184 | bytes 3469316 | tf_op jit(solution)/shard_map/pallas_call | solution.py:346
  16.8 1.2 %collective-permute-done.5.got_ref = bf16[2,16,768]{2,1,0:T(8,128)(2,1)S(1)} collective-permute-done((bf16[2,16,768]{2,1,0:T(8,128)(2,1)S(1)}, bf16[2,16,768]{2,1,0:T(8,128)(2,1)S(1)}, u32[]{:S(2)}, u32[]{:S(2)}) %collective-permute-start.5) | collective-permute-done | bytes 49184 | tf_op jit(solution)/shard_map/ppermute | solution.py:385
  18.0 0.7 %shard_map.101 = (bf16[2,16,768]{2,1,0:T(8,128)(2,1)S(1)}, bf16[2,24,640]{2,1,0:T(8,128)(2,1)S(1)}, bf16[96,1024]{1,0:T(8,128)(2,1)S(1)}) custom-call(s32[1]{0:T(128)} %bitcast.row_ref, s32[8,128]{1,0:T(8,128)S(1)} %get-tuple-element.28.code_ref.code0_ref, bf16[2,1024,128]{2,1,0:T(8,128)(2,1)S(1)} %copy-done.1, bf16[640,1024]{1,0:T(8,128)(2,1)S(1)} %bitcast.6, ...), custom_call_target="tpu_custom_call" | custom-call | flops 201326592 | bytes 2281476 | tf_op jit(solution)/shard_map/pallas_call | solution.py:346
  18.7 0.9 %collective-permute-start.6 = (bf16[2,16,768]{2,1,0:T(8,128)(2,1)S(1)}, bf16[2,16,768]{2,1,0:T(8,128)(2,1)S(1)}, u32[]{:S(2)}, u32[]{:S(2)}) collective-permute-start(bf16[2,16,768]{2,1,0:T(8,128)(2,1)S(1)} %get-tuple-element.47), channel_id=1, source_target_pairs={{0,16},{1,17},{2,18},{3,19},{4,20},{5,21},{6,22},{7,23},{8,24},{9,... | collective-permute-start | bytes 147464 | tf_op jit(solution)/shard_map/ppermute | solution.py:385
  19.7 2.4 %shard_map.102 = (f32[64,1024]{1,0:T(8,128)S(1)}, bf16[4,16,640]{2,1,0:T(8,128)(2,1)S(1)}, bf16[2,16,4,1024]{3,2,1,0:T(4,128)(2,1)}) custom-call(s32[1]{0:T(128)} %bitcast.row_ref, s32[8,128]{1,0:T(8,128)S(1)} %get-tuple-element.28.code_ref.code0_ref, s32[8,128]{1,0:T(8,128)S(1)} %get-tuple-element.31.code_ref.code1_ref, ...), custom_call_target="tpu_custom_call" | custom-call | flops 402653184 | bytes 3469316 | tf_op jit(solution)/shard_map/pallas_call | solution.py:346
  22.1 0.8 %collective-permute-done.6.got_ref = bf16[2,16,768]{2,1,0:T(8,128)(2,1)S(1)} collective-permute-done((bf16[2,16,768]{2,1,0:T(8,128)(2,1)S(1)}, bf16[2,16,768]{2,1,0:T(8,128)(2,1)S(1)}, u32[]{:S(2)}, u32[]{:S(2)}) %collective-permute-start.6) | collective-permute-done | bytes 49184 | tf_op jit(solution)/shard_map/ppermute | solution.py:385
  22.9 1.6 %shard_map.103 = (bf16[4,8,2560]{2,1,0:T(8,128)(2,1)}, bf16[2,16,4,1024]{3,2,1,0:T(4,128)(2,1)}) custom-call(s32[1]{0:T(128)} %bitcast.row_ref, s32[8,128]{1,0:T(8,128)S(1)} %get-tuple-element.28.code_ref.code0_ref, bf16[2,1024,128]{2,1,0:T(8,128)(2,1)S(1)} %copy-done.1, bf16[640,1024]{1,0:T(8,128)(2,1)S(1)} %bitcast.8, ...), custom_call_target="tpu_custom_call", output_to_operand_aliasing={{1}: (7, {})} | custom-call | flops 201326592 | bytes 2494468 | tf_op jit(solution)/shard_map/pallas_call | solution.py:346
  (5 shorter events, 0.0 us)
Async XLA Ops:
  0.6 10.4 %copy-start.3 = (bf16[2,16,4,1024]{3,2,1,0:T(4,128)(2,1)S(1)}, bf16[2,16,4,1024]{3,2,1,0:T(4,128)(2,1)}, u32[]{:S(2)}) copy-start(bf16[2,16,4,1024]{3,2,1,0:T(4,128)(2,1)} %state_ref.3) | copy-start | bytes 786436
  0.6 10.4 %copy-start.4 = (s32[2,8,2]{1,2,0:T(2,128)S(1)}, s32[2,8,2]{1,2,0:T(2,128)}, u32[]{:S(2)}) copy-start(s32[2,8,2]{1,2,0:T(2,128)} %param.11) | copy-start | bytes 388
  0.7 10.4 %copy-start.5 = (s32[2,8]{1,0:T(2,128)S(1)}, s32[2,8]{1,0:T(2,128)}, u32[]{:S(2)}) copy-start(s32[2,8]{1,0:T(2,128)} %iidx_ref.3) | copy-start | bytes 196
  0.7 10.4 %copy-start.6 = (s32[2]{0:T(128)S(1)}, s32[2]{0:T(128)}, u32[]{:S(2)}) copy-start(s32[2]{0:T(128)} %band_ref.3) | copy-start | bytes 28
  0.7 10.9 %copy-start.2 = (bf16[2,2048,128]{2,1,0:T(8,128)(2,1)S(1)}, bf16[2,2048,128]{2,1,0:T(8,128)(2,1)}, u32[]{:S(2)}) copy-start(bf16[2,2048,128]{2,1,0:T(8,128)(2,1)} %coup_ref.7) | copy-start | bytes 3145732
  1.8 9.8 %copy-start = (bf16[1,640,1024]{2,1,0:T(8,128)(2,1)S(1)}, bf16[1,640,1024]{2,1,0:T(8,128)(2,1)}, u32[]{:S(2)}) copy-start(bf16[1,640,1024]{2,1,0:T(8,128)(2,1)} %param.14) | copy-start | bytes 3932164
  1.9 9.8 %copy-start.1 = (bf16[2,1024,128]{2,1,0:T(8,128)(2,1)S(1)}, bf16[2,1024,128]{2,1,0:T(8,128)(2,1)}, u32[]{:S(2)}) copy-start(bf16[2,1024,128]{2,1,0:T(8,128)(2,1)} %inp_ref.11) | copy-start | bytes 1572868
  1.9 9.2 %collective-permute-start = (bf16[4,8,1024]{2,1,0:T(8,128)(2,1)S(1)}, bf16[4,8,1024]{2,1,0:T(8,128)(2,1)S(1)}, u32[]{:S(2)}, u32[]{:S(2)}) collective-permute-start(bf16[4,8,1024]{2,1,0:T(8,128)(2,1)S(1)} %get-tuple-element.26), channel_id=1, source_target_pairs={{0,1},{1,2},{2,3},{3,4},{4,5},{5,6},{6,7},{7,8},{8,9},{9,10},{10,1... | collective-permute-start | bytes 196616 | tf_op jit(solution)/shard_map/ppermute | solution.py:385
  2.4 8.7 %collective-permute-start.1 = (bf16[8,1536]{1,0:T(8,128)(2,1)S(1)}, bf16[8,1536]{1,0:T(8,128)(2,1)S(1)}, u32[]{:S(2)}, u32[]{:S(2)}) collective-permute-start(bf16[8,1536]{1,0:T(8,128)(2,1)S(1)} %get-tuple-element.27), channel_id=1, source_target_pairs={{0,17},{1,18},{2,19},{3,20},{4,21},{5,22},{6,23},{7,24},{8,25},{9,... | collective-permute-start | bytes 73736 | tf_op jit(solution)/shard_map/ppermute | solution.py:385
  6.1 5.2 %collective-permute-start.2 = (bf16[2,16,640]{2,1,0:T(8,128)(2,1)S(1)}, bf16[2,16,640]{2,1,0:T(8,128)(2,1)S(1)}, u32[]{:S(2)}, u32[]{:S(2)}) collective-permute-start(bf16[2,16,640]{2,1,0:T(8,128)(2,1)S(1)} %get-tuple-element.29), channel_id=1, source_target_pairs={{0,16},{1,17},{2,18},{3,19},{4,20},{5,21},{6,22},{7,23},{8,24},{9,... | collective-permute-start | bytes 122888 | tf_op jit(solution)/shard_map/ppermute | solution.py:385
  6.6 5.0 %collective-permute-start.3 = (bf16[4,8,1024]{2,1,0:T(8,128)(2,1)S(1)}, bf16[4,8,1024]{2,1,0:T(8,128)(2,1)S(1)}, u32[]{:S(2)}, u32[]{:S(2)}) collective-permute-start(bf16[4,8,1024]{2,1,0:T(8,128)(2,1)S(1)} %get-tuple-element.33), channel_id=1, source_target_pairs={{0,15},{1,0},{2,1},{3,2},{4,3},{5,4},{6,5},{7,6},{8,7},{9,8},{10,9... | collective-permute-start | bytes 196616 | tf_op jit(solution)/shard_map/ppermute | solution.py:385
  9.1 3.8 %collective-permute-start.4 = (bf16[8,512]{1,0:T(8,128)(2,1)S(1)}, bf16[8,512]{1,0:T(8,128)(2,1)S(1)}, u32[]{:S(2)}, u32[]{:S(2)}) collective-permute-start(bf16[8,512]{1,0:T(8,128)(2,1)S(1)} %get-tuple-element.34), channel_id=1, source_target_pairs={{0,31},{1,16},{2,17},{3,18},{4,19},{5,20},{6,21},{7,22},{8,23},{9,... | collective-permute-start | bytes 24584 | tf_op jit(solution)/shard_map/ppermute | solution.py:385
  13.9 4.2 %collective-permute-start.5 = (bf16[2,16,768]{2,1,0:T(8,128)(2,1)S(1)}, bf16[2,16,768]{2,1,0:T(8,128)(2,1)S(1)}, u32[]{:S(2)}, u32[]{:S(2)}) collective-permute-start(bf16[2,16,768]{2,1,0:T(8,128)(2,1)S(1)} %get-tuple-element.41), channel_id=1, source_target_pairs={{0,16},{1,17},{2,18},{3,19},{4,20},{5,21},{6,22},{7,23},{8,24},{9,... | collective-permute-start | bytes 147464 | tf_op jit(solution)/shard_map/ppermute | solution.py:385
  18.7 4.2 %collective-permute-start.6 = (bf16[2,16,768]{2,1,0:T(8,128)(2,1)S(1)}, bf16[2,16,768]{2,1,0:T(8,128)(2,1)S(1)}, u32[]{:S(2)}, u32[]{:S(2)}) collective-permute-start(bf16[2,16,768]{2,1,0:T(8,128)(2,1)S(1)} %get-tuple-element.47), channel_id=1, source_target_pairs={{0,16},{1,17},{2,18},{3,19},{4,20},{5,21},{6,22},{7,23},{8,24},{9,... | collective-permute-start | bytes 147464 | tf_op jit(solution)/shard_map/ppermute | solution.py:385

commit v3 on v1

--- a/solution.py
+++ b/solution.py
@@ -189,10 +189,7 @@
     if edge:
         send_edge(r, state, read_ref, *outs)
         return
-    outs[1][...] = state
-    pred = lax.dot_general(state, read_ref[...], NT, preferred_element_type=F32)
-    for d in range(4):
-        outs[0][d] = latitude(pred, d).astype(BF)
+    outs[0][...] = state
 
 
 def narrowed(s):
@@ -200,7 +197,7 @@
     return jnp.concatenate([s[res * per + MEM : (res + 1) * per - MEM] for res in range(4)], axis=0)
 
 
-def shadow_kernel(last, slots, row_ref, band_ref, cidx_ref, iidx_ref, coup_ref, inp_ref, read_ref, *rest):
+def shadow_kernel(second, last, slots, row_ref, band_ref, cidx_ref, iidx_ref, coup_ref, inp_ref, read_ref, *rest):
     rest = list(rest)
 
     def take(n):
@@ -209,7 +206,7 @@
         return got
 
     edge_refs, s_refs = take(slots), take(slots)
-    far_refs = take(2 * (2 - slots))
+    far_refs = take((1 if second else 2) * (2 - slots))
     pre_refs = take(slots)
     out_far = take(2 * (2 - slots))
     xs_ref, in_ref = take(2)
@@ -224,9 +221,12 @@
             xs_ref[2 + 4 * r + 2 * r + d] = edge_refs[slot][d].astype(F32)
             xs_ref[2 + 4 * r + 2 * (1 - r) + d] = latitude(pred, d).astype(BF).astype(F32)
     if far_refs:
+        s_refs = [s_refs[0], far_refs[-1]]
+        if second:
+            pred = lax.dot_general(far_refs[0][...], read_ref[...], NT, preferred_element_type=F32)
         for d in range(4):
-            xs_ref[2 + 4 * rows_at[1] + d] = far_refs[0][d].astype(F32)
-        s_refs = [s_refs[0], far_refs[1]]
+            lat = latitude(pred, d).astype(BF) if second else far_refs[0][d]
+            xs_ref[2 + 4 * rows_at[1] + d] = lat.astype(F32)
     if last:
         short_refs = take(2)
         for slot in range(2):
@@ -404,11 +404,11 @@
         operands.append((from_right, VM))
         if edge:
             operands.append((from_dright[slot], VM))
-            operands += [(x, VM) for x in far[1:]]
+            operands += [(x, VM) for x in far]
         got = call(
-            functools.partial(first_kernel, slot, edge, len(far[1:])),
-            send_out if edge else [bf(4, wide, CHUNK), bf(rows, units)],
-            [VM] * (3 if edge else 2),
+            functools.partial(first_kernel, slot, edge, len(far)),
+            send_out if edge else [bf(rows, units)],
+            [VM] * (3 if edge else 1),
             [padded, vm((rows, units)), vm((rows, 16 * CELL))],
             operands,
             flops if edge else 0,
@@ -430,7 +430,7 @@
             specs += [VM, HB if last else VM]
             scratch += stage if last else []
         shadow = call(
-            functools.partial(shadow_kernel, last, slots),
+            functools.partial(shadow_kernel, step == 1, last, slots),
             out,
             specs,
             scratch,

time: 24.4 us -> 24.1 us (0.988)
  Pallas kernels: 10.5 us -> 10.1 us
    pallas_call x9, Pallas kernels: 10.5 us -> 10.1 us  [call(): pl.pallas_call(kernel, out_shape=out_shape, in_specs=[s for _, s in opera...]
    ppermute x7, starting transfers between devices: 11.7 us -> 11.9 us  [send(): return lax.ppermute(x, ('lat', 'lon'), pairs)]
  transfers between devices with their start and end apart: 7 -> 7, of which waited for: 3 -> 4; matrix products, arithmetic and copies ran while one was open for 0% -> 0% of each run, Pallas kernels for 24% -> 23%
where the time goes in v3:
time: 24.1 us; the launch traced here: 24 us
  starting transfers between devices  11.9 us (49%)
  Pallas kernels  10.1 us (42%)
  waiting for transfers between devices  1.14 us (5%)
  between operations  0.82 us (3%)
    ppermute x7, starting transfers between devices, send(): return lax.ppermute(x, ('lat', 'lon'), pairs)  11.9 us
    pallas_call x9, Pallas kernels, call(): pl.pallas_call(kernel, out_shape=out_shape, in_specs=[s for _, s in opera...  10.1 us
    ppermute x7, waiting for transfers between devices, send(): return lax.ppermute(x, ('lat', 'lon'), pairs)  1.14 us
  transfers between devices with their start and end apart: 7, of which 4 were waited for; matrix products, arithmetic and copies ran while one was open for 0% of the time, Pallas kernels for 23%

profile of v3, /device:TPU:0, one launch (start us, length us, event | category | flops | bytes accessed | tf_op | source)
XLA Modules:
  0.0 24.0 jit_solution(10659277778369175294)
XLA Ops:
  0.6 0.0 copy-start.6
  0.6 0.0 copy-start.2
  0.7 1.2 %shard_map.95 = (bf16[4,8,1024]{2,1,0:T(8,128)(2,1)S(1)}, bf16[4,8,1024]{2,1,0:T(8,128)(2,1)S(1)}, bf16[8,16,640]{2,1,0:T(8,128)(2,1)S(1)}, bf16[8,1536]{1,0:T(8...) custom-call(s32[1]{0:T(128)} %bitcast.row_ref, bf16[4,8,2560]{2,1,0:T(8,128)(2,1)} %field_hbm.1, ...), custom_call_target="tpu_custom_call" | custom-call | flops 10000000000 | bytes 425988 | tf_op jit(solution)/shard_map/pallas_call | solution.py:319
  1.8 0.0 copy-start
  1.8 0.0 copy-start.1
  1.8 0.0 copy-start.3
  1.9 0.0 copy-start.4
  1.9 0.0 copy-start.5
  1.9 0.5 %collective-permute-start = (bf16[4,8,1024]{2,1,0:T(8,128)(2,1)S(1)}, bf16[4,8,1024]{2,1,0:T(8,128)(2,1)S(1)}, u32[]{:S(2)}, u32[]{:S(2)}) collective-permute-start(bf16[4,8,1024]{2,1,0:T(8,128)(2,1)S(1)} %get-tuple-element.21), channel_id=1, source_target_pairs={{0,1},{1,2},{2,3},{3,4},{4,5},{5,6},{6,7},{7,8},{8,9},{9,10},{10,1... | collective-permute-start | bytes 196616 | tf_op jit(solution)/shard_map/ppermute | solution.py:358
  2.4 3.7 %collective-permute-start.1 = (bf16[8,1536]{1,0:T(8,128)(2,1)S(1)}, bf16[8,1536]{1,0:T(8,128)(2,1)S(1)}, u32[]{:S(2)}, u32[]{:S(2)}) collective-permute-start(bf16[8,1536]{1,0:T(8,128)(2,1)S(1)} %get-tuple-element.22), channel_id=1, source_target_pairs={{0,17},{1,18},{2,19},{3,20},{4,21},{5,22},{6,23},{7,24},{8,25},{9,... | collective-permute-start | bytes 73736 | tf_op jit(solution)/shard_map/ppermute | solution.py:358
  6.1 0.5 %collective-permute-start.2 = (bf16[2,16,640]{2,1,0:T(8,128)(2,1)S(1)}, bf16[2,16,640]{2,1,0:T(8,128)(2,1)S(1)}, u32[]{:S(2)}, u32[]{:S(2)}) collective-permute-start(bf16[2,16,640]{2,1,0:T(8,128)(2,1)S(1)} %get-tuple-element.23), channel_id=1, source_target_pairs={{0,16},{1,17},{2,18},{3,19},{4,20},{5,21},{6,22},{7,23},{8,24},{9,... | collective-permute-start | bytes 122888 | tf_op jit(solution)/shard_map/ppermute | solution.py:358
  6.6 2.4 %collective-permute-start.3 = (bf16[4,8,1024]{2,1,0:T(8,128)(2,1)S(1)}, bf16[4,8,1024]{2,1,0:T(8,128)(2,1)S(1)}, u32[]{:S(2)}, u32[]{:S(2)}) collective-permute-start(bf16[4,8,1024]{2,1,0:T(8,128)(2,1)S(1)} %get-tuple-element.24), channel_id=1, source_target_pairs={{0,15},{1,0},{2,1},{3,2},{4,3},{5,4},{6,5},{7,6},{8,7},{9,8},{10,9... | collective-permute-start | bytes 196616 | tf_op jit(solution)/shard_map/ppermute | solution.py:358
  9.1 1.8 %collective-permute-start.4 = (bf16[8,512]{1,0:T(8,128)(2,1)S(1)}, bf16[8,512]{1,0:T(8,128)(2,1)S(1)}, u32[]{:S(2)}, u32[]{:S(2)}) collective-permute-start(bf16[8,512]{1,0:T(8,128)(2,1)S(1)} %get-tuple-element.25), channel_id=1, source_target_pairs={{0,31},{1,16},{2,17},{3,18},{4,19},{5,20},{6,21},{7,22},{8,23},{9,... | collective-permute-start | bytes 24584 | tf_op jit(solution)/shard_map/ppermute | solution.py:358
  10.9 0.2 collective-permute-done.1.rest_1_.rest_0_
  11.1 0.0 collective-permute-done.rest_0_.fl_ref
  11.1 0.0 copy-done.6
  11.1 0.0 collective-permute-done.2.rest_0_.rest_1_
  11.2 0.0 collective-permute-done.3.rest_1_.rest_2_
  11.2 0.0 copy-done.2
  11.2 0.0 copy-done
  11.2 0.0 copy-done.1
  11.2 0.8 %shard_map.98.rest_4_.rest_2_ = bf16[96,1024]{1,0:T(8,128)(2,1)S(1)} custom-call(s32[1]{0:T(128)} %bitcast.row_ref, s32[2]{0:T(128)S(1)} %copy-done.5, s32[2,2,8]{2,1,0:T(2,128)S(1)} %bitcast.9, s32[2,8]{1,0:T(2,128)S(1)} %copy-done.3, bf16[2,2048,128]{2,1,0:T(8,128)(2,1)S(1)} %copy-done.2, bf16[2,1024,128]{2,1,0:T(8,128)(2,1)S(1)} %copy-done.1, ...), custom_call_target="tpu_custom_call" | custom-call | bytes 3350732 | tf_op jit(solution)/shard_map/pallas_call | solution.py:319
  12.0 0.2 collective-permute-done.4.rest_3_
  12.3 1.1 %shard_map.99 = (bf16[2,16,768]{2,1,0:T(8,128)(2,1)S(1)}, bf16[2,24,640]{2,1,0:T(8,128)(2,1)S(1)}, bf16[96,1024]{1,0:T(8,128)(2,1)S(1)}) custom-call(s32[1]{0:T(128)} %bitcast.row_ref, s32[2]{0:T(128)S(1)} %copy-done.5, s32[2,2,8]{2,1,0:T(2,128)S(1)} %bitcast.10, s32[2,8]{1,0:T(2,128)S(1)} %copy-done.3, bf16[2,2048,128]{2,1,0:T(8,128)(2,1)S(1)} %copy-done.2, ...), custom_call_target="tpu_custom_call" | custom-call | flops 201326592 | bytes 3580108 | tf_op jit(solution)/shard_map/pallas_call | solution.py:319
  13.3 1.4 %collective-permute-start.5 = (bf16[2,16,768]{2,1,0:T(8,128)(2,1)S(1)}, bf16[2,16,768]{2,1,0:T(8,128)(2,1)S(1)}, u32[]{:S(2)}, u32[]{:S(2)}) collective-permute-start(bf16[2,16,768]{2,1,0:T(8,128)(2,1)S(1)} %get-tuple-element.29), channel_id=1, source_target_pairs={{0,16},{1,17},{2,18},{3,19},{4,20},{5,21},{6,22},{7,23},{8,24},{9,... | collective-permute-start | bytes 147464 | tf_op jit(solution)/shard_map/ppermute | solution.py:358
  14.8 2.1 %shard_map.100 = (f32[96,1024]{1,0:T(8,128)S(1)}, bf16[4,24,640]{2,1,0:T(8,128)(2,1)S(1)}, bf16[96,1024]{1,0:T(8,128)(2,1)S(1)}) custom-call(s32[1]{0:T(128)} %bitcast.row_ref, s32[2]{0:T(128)S(1)} %copy-done.5, s32[2,2,8]{2,1,0:T(2,128)S(1)} %bitcast.11, s32[2,8]{1,0:T(2,128)S(1)} %copy-done.3, bf16[2,2048,128]{2,1,0:T(8,128)(2,1)S(1)} %copy-done.2, ...), custom_call_target="tpu_custom_call" | custom-call | flops 402653184 | bytes 3338444 | tf_op jit(solution)/shard_map/pallas_call | solution.py:319
  16.9 0.6 %collective-permute-done.5.got_ref = bf16[2,16,768]{2,1,0:T(8,128)(2,1)S(1)} collective-permute-done((bf16[2,16,768]{2,1,0:T(8,128)(2,1)S(1)}, bf16[2,16,768]{2,1,0:T(8,128)(2,1)S(1)}, u32[]{:S(2)}, u32[]{:S(2)}) %collective-permute-start.5) | collective-permute-done | bytes 49184 | tf_op jit(solution)/shard_map/ppermute | solution.py:358
  17.5 0.7 %shard_map.101 = (bf16[2,16,768]{2,1,0:T(8,128)(2,1)S(1)}, bf16[2,24,640]{2,1,0:T(8,128)(2,1)S(1)}, bf16[96,1024]{1,0:T(8,128)(2,1)S(1)}) custom-call(s32[1]{0:T(128)} %bitcast.row_ref, s32[2]{0:T(128)S(1)} %copy-done.5, s32[2,8]{1,0:T(2,128)S(1)} %copy-done.3, bf16[2,1024,128]{2,1,0:T(8,128)(2,1)S(1)} %copy-done.1, bf16[640,1024]{1,0:T(8,128)(2,1)S(1)} %bitcast.6, ...), custom_call_target="tpu_custom_call" | custom-call | flops 201326592 | bytes 2277452 | tf_op jit(solution)/shard_map/pallas_call | solution.py:319
  18.2 1.5 %collective-permute-start.6 = (bf16[2,16,768]{2,1,0:T(8,128)(2,1)S(1)}, bf16[2,16,768]{2,1,0:T(8,128)(2,1)S(1)}, u32[]{:S(2)}, u32[]{:S(2)}) collective-permute-start(bf16[2,16,768]{2,1,0:T(8,128)(2,1)S(1)} %get-tuple-element.35), channel_id=1, source_target_pairs={{0,16},{1,17},{2,18},{3,19},{4,20},{5,21},{6,22},{7,23},{8,24},{9,... | collective-permute-start | bytes 147464 | tf_op jit(solution)/shard_map/ppermute | solution.py:358
  19.7 2.6 %shard_map.102 = (f32[64,1024]{1,0:T(8,128)S(1)}, bf16[4,16,640]{2,1,0:T(8,128)(2,1)S(1)}, bf16[2,16,4,1024]{3,2,1,0:T(4,128)(2,1)}) custom-call(s32[1]{0:T(128)} %bitcast.row_ref, s32[2]{0:T(128)S(1)} %copy-done.5, s32[2,2,8]{2,1,0:T(2,128)S(1)} %bitcast.12, s32[2,8]{1,0:T(2,128)S(1)} %copy-done.3, bf16[2,2048,128]{2,1,0:T(8,128)(2,1)S(1)} %copy-done.2, ...), custom_call_target="tpu_custom_call" | custom-call | flops 402653184 | bytes 3461324 | tf_op jit(solution)/shard_map/pallas_call | solution.py:319
  22.2 0.1 collective-permute-done.6.got_ref
  22.4 1.6 %shard_map.103 = (bf16[4,8,2560]{2,1,0:T(8,128)(2,1)}, bf16[2,16,4,1024]{3,2,1,0:T(4,128)(2,1)}) custom-call(s32[1]{0:T(128)} %bitcast.row_ref, s32[2]{0:T(128)S(1)} %copy-done.5, s32[2,8]{1,0:T(2,128)S(1)} %copy-done.3, bf16[2,1024,128]{2,1,0:T(8,128)(2,1)S(1)} %copy-done.1, bf16[640,1024]{1,0:T(8,128)(2,1)S(1)} %bitcast.8, ...), custom_call_target="tpu_custom_call", output_to_operand_aliasing={{1}: (8, {})} | custom-call | flops 201326592 | bytes 2490444 | tf_op jit(solution)/shard_map/pallas_call | solution.py:319
  (5 shorter events, 0.1 us)
Async XLA Ops:
  0.6 10.4 %copy-start.6 = (bf16[2,16,4,1024]{3,2,1,0:T(4,128)(2,1)S(1)}, bf16[2,16,4,1024]{3,2,1,0:T(4,128)(2,1)}, u32[]{:S(2)}) copy-start(bf16[2,16,4,1024]{3,2,1,0:T(4,128)(2,1)} %state_ref.3) | copy-start | bytes 786436
  0.6 10.5 %copy-start.2 = (bf16[2,2048,128]{2,1,0:T(8,128)(2,1)S(1)}, bf16[2,2048,128]{2,1,0:T(8,128)(2,1)}, u32[]{:S(2)}) copy-start(bf16[2,2048,128]{2,1,0:T(8,128)(2,1)} %coup_ref.7) | copy-start | bytes 3145732
  1.8 9.4 %copy-start = (bf16[1,640,1024]{2,1,0:T(8,128)(2,1)S(1)}, bf16[1,640,1024]{2,1,0:T(8,128)(2,1)}, u32[]{:S(2)}) copy-start(bf16[1,640,1024]{2,1,0:T(8,128)(2,1)} %param.14) | copy-start | bytes 3932164
  1.8 9.4 %copy-start.1 = (bf16[2,1024,128]{2,1,0:T(8,128)(2,1)S(1)}, bf16[2,1024,128]{2,1,0:T(8,128)(2,1)}, u32[]{:S(2)}) copy-start(bf16[2,1024,128]{2,1,0:T(8,128)(2,1)} %inp_ref.11) | copy-start | bytes 1572868
  1.8 9.4 %copy-start.3 = (s32[2,8]{1,0:T(2,128)S(1)}, s32[2,8]{1,0:T(2,128)}, u32[]{:S(2)}) copy-start(s32[2,8]{1,0:T(2,128)} %iidx_ref.11) | copy-start | bytes 196
  1.9 9.4 %copy-start.4 = (s32[2,8,2]{1,2,0:T(2,128)S(1)}, s32[2,8,2]{1,2,0:T(2,128)}, u32[]{:S(2)}) copy-start(s32[2,8,2]{1,2,0:T(2,128)} %param.11) | copy-start | bytes 388
  1.9 9.4 %copy-start.5 = (s32[2]{0:T(128)S(1)}, s32[2]{0:T(128)}, u32[]{:S(2)}) copy-start(s32[2]{0:T(128)} %band_ref.11) | copy-start | bytes 28
  1.9 9.2 %collective-permute-start = (bf16[4,8,1024]{2,1,0:T(8,128)(2,1)S(1)}, bf16[4,8,1024]{2,1,0:T(8,128)(2,1)S(1)}, u32[]{:S(2)}, u32[]{:S(2)}) collective-permute-start(bf16[4,8,1024]{2,1,0:T(8,128)(2,1)S(1)} %get-tuple-element.21), channel_id=1, source_target_pairs={{0,1},{1,2},{2,3},{3,4},{4,5},{5,6},{6,7},{7,8},{8,9},{9,10},{10,1... | collective-permute-start | bytes 196616 | tf_op jit(solution)/shard_map/ppermute | solution.py:358
  2.4 8.7 %collective-permute-start.1 = (bf16[8,1536]{1,0:T(8,128)(2,1)S(1)}, bf16[8,1536]{1,0:T(8,128)(2,1)S(1)}, u32[]{:S(2)}, u32[]{:S(2)}) collective-permute-start(bf16[8,1536]{1,0:T(8,128)(2,1)S(1)} %get-tuple-element.22), channel_id=1, source_target_pairs={{0,17},{1,18},{2,19},{3,20},{4,21},{5,22},{6,23},{7,24},{8,25},{9,... | collective-permute-start | bytes 73736 | tf_op jit(solution)/shard_map/ppermute | solution.py:358
  6.1 5.0 %collective-permute-start.2 = (bf16[2,16,640]{2,1,0:T(8,128)(2,1)S(1)}, bf16[2,16,640]{2,1,0:T(8,128)(2,1)S(1)}, u32[]{:S(2)}, u32[]{:S(2)}) collective-permute-start(bf16[2,16,640]{2,1,0:T(8,128)(2,1)S(1)} %get-tuple-element.23), channel_id=1, source_target_pairs={{0,16},{1,17},{2,18},{3,19},{4,20},{5,21},{6,22},{7,23},{8,24},{9,... | collective-permute-start | bytes 122888 | tf_op jit(solution)/shard_map/ppermute | solution.py:358
  6.6 4.5 %collective-permute-start.3 = (bf16[4,8,1024]{2,1,0:T(8,128)(2,1)S(1)}, bf16[4,8,1024]{2,1,0:T(8,128)(2,1)S(1)}, u32[]{:S(2)}, u32[]{:S(2)}) collective-permute-start(bf16[4,8,1024]{2,1,0:T(8,128)(2,1)S(1)} %get-tuple-element.24), channel_id=1, source_target_pairs={{0,15},{1,0},{2,1},{3,2},{4,3},{5,4},{6,5},{7,6},{8,7},{9,8},{10,9... | collective-permute-start | bytes 196616 | tf_op jit(solution)/shard_map/ppermute | solution.py:358
  9.1 3.2 %collective-permute-start.4 = (bf16[8,512]{1,0:T(8,128)(2,1)S(1)}, bf16[8,512]{1,0:T(8,128)(2,1)S(1)}, u32[]{:S(2)}, u32[]{:S(2)}) collective-permute-start(bf16[8,512]{1,0:T(8,128)(2,1)S(1)} %get-tuple-element.25), channel_id=1, source_target_pairs={{0,31},{1,16},{2,17},{3,18},{4,19},{5,20},{6,21},{7,22},{8,23},{9,... | collective-permute-start | bytes 24584 | tf_op jit(solution)/shard_map/ppermute | solution.py:358
  13.3 4.2 %collective-permute-start.5 = (bf16[2,16,768]{2,1,0:T(8,128)(2,1)S(1)}, bf16[2,16,768]{2,1,0:T(8,128)(2,1)S(1)}, u32[]{:S(2)}, u32[]{:S(2)}) collective-permute-start(bf16[2,16,768]{2,1,0:T(8,128)(2,1)S(1)} %get-tuple-element.29), channel_id=1, source_target_pairs={{0,16},{1,17},{2,18},{3,19},{4,20},{5,21},{6,22},{7,23},{8,24},{9,... | collective-permute-start | bytes 147464 | tf_op jit(solution)/shard_map/ppermute | solution.py:358
  18.2 4.2 %collective-permute-start.6 = (bf16[2,16,768]{2,1,0:T(8,128)(2,1)S(1)}, bf16[2,16,768]{2,1,0:T(8,128)(2,1)S(1)}, u32[]{:S(2)}, u32[]{:S(2)}) collective-permute-start(bf16[2,16,768]{2,1,0:T(8,128)(2,1)S(1)} %get-tuple-element.35), channel_id=1, source_target_pairs={{0,16},{1,17},{2,18},{3,19},{4,20},{5,21},{6,22},{7,23},{8,24},{9,... | collective-permute-start | bytes 147464 | tf_op jit(solution)/shard_map/ppermute | solution.py:358

commit v4 on v3

--- a/solution.py
+++ b/solution.py
@@ -122,13 +122,16 @@
     return pl.multiple_of(jnp.clip(index, 0, ref.shape[1] // BLK - 1) * BLK, BLK)
 
 
-def block_pre(b, band, s_ref, in_ref, cidx, iidx, coup_ref, inp_ref):
+def block_pre(b, band, s_ref, in_ref, cidx, iidx, coup_ref, inp_ref, other=None):
     pieces = []
     mats = [coup_ref[band, (2 * b + k) * BLK : (2 * b + k + 1) * BLK, :] for k in range(2)]
     mats.append(inp_ref[band, b * BLK : (b + 1) * BLK, :])
     for k in range(2):
         pieces.append(s_ref[:, pl.ds(block_at(of_band(band, cidx, k, b), s_ref), BLK)])
     pieces.append(in_ref[:, pl.ds(block_at(of_band(band, iidx, b), in_ref), BLK)])
+    if other is not None:
+        used, ref, at = other
+        pieces[2] = jnp.where(used, ref[:, pl.ds(at, BLK)], pieces[2])
     return lax.dot_general(jnp.concatenate(pieces, axis=1), jnp.concatenate(mats, axis=1), NT, preferred_element_type=F32)
 
 
@@ -145,51 +148,65 @@
         edge_ref[d] = row.astype(BF)
 
 
-def first_kernel(slot, edge, behind, row_ref, band_ref, cidx_ref, iidx_ref, coup_ref, inp_ref, read_ref, own_ref, s0_ref, fl_ref, *rest):
-    rest = list(rest)
-    r = row_of(slot, row_ref)
-    if edge:
-        dl_ref, lat_ref, fr_ref, dr_ref = rest[:4]
-        del rest[: 4 + behind]
-    else:
-        fr_ref = rest[1]
-        del rest[:2]
-    outs, (xs_ref, s_ref, in_ref) = rest[:-3], rest[-3:]
+def widen(own, left, right):
     fill = jnp.zeros((MEM, CHUNK - HALF), F32)
-
-    def widen(own, left, right):
-        left = jnp.concatenate([fill, left.astype(F32)], axis=1)
-        right = jnp.concatenate([right.astype(F32), fill], axis=1)
-        return jnp.concatenate([left, own.astype(F32), right], axis=0)
-
+    left = jnp.concatenate([fill, left.astype(F32)], axis=1)
+    right = jnp.concatenate([right.astype(F32), fill], axis=1)
+    return jnp.concatenate([left, own.astype(F32), right], axis=0)
+
+
+def first_kernel(slots, row_ref, band_ref, cidx_ref, iidx_ref, coup_ref, inp_ref, own_ref, s0_ref, s1_ref, fl_ref, *rest):
+    fr_ref = rest[slots]
+    outs = rest[slots + 1 : -3]
+    xs_ref, s_ref, in_ref = rest[-3:]
+    for k in range(2):
+        xs_ref[k] = jnp.zeros(xs_ref.shape[1:], F32)
+        xs_ref[10 + k] = jnp.zeros(xs_ref.shape[1:], F32)
     for d in range(8):
         at, lane = (d % 2) * MEM, (d // 2 % 2) * HALF
         left = fl_ref[2 + d // 4, at : at + MEM, lane : lane + HALF]
         right = fr_ref[2 + d // 4, at : at + MEM, lane : lane + HALF]
         xs_ref[2 + d] = widen(own_ref[d], left, right)
+    empty = jnp.zeros((MEM, s_ref.shape[1]), F32)
+    bands, cidx, iidx = band_ref[...], cidx_ref[...], iidx_ref[...]
+    for slot, src in ((1, s1_ref), (0, s0_ref)):
+        r = row_of(slot, row_ref)
+        per = src.shape[0] // 4
+        rows = []
+        for res in range(4):
+            rows.append(fl_ref[r, (res - 2) * MEM : (res - 1) * MEM].astype(F32) if res >= 2 else empty)
+            rows.append(src[res * per : (res + 1) * per].astype(F32))
+            rows.append(fr_ref[r, res * MEM : (res + 1) * MEM].astype(F32) if res < 2 else empty)
+        states = jnp.concatenate(rows, axis=0).astype(BF)
+        inputs = windows([xs_ref[4 * r + d] for d in range(8)], False)
+        if slot < slots:
+            outs[2 * slot][...] = states
+            outs[2 * slot + 1][...] = inputs
+            continue
+        s_ref[...] = states
+        in_ref[...] = inputs
+        band = jnp.where(r == 0, bands[0], bands[1])
+        pres = [block_pre(b, band, s_ref, in_ref, cidx, iidx, coup_ref, inp_ref) for b in range(iidx_ref.shape[1])]
+        outs[2 * slots][...] = jnp.concatenate([jnp.tanh(p).astype(BF) for p in pres], axis=1)
+
+
+def first_edge_kernel(slot, row_ref, band_ref, cidx_ref, iidx_ref, coup_ref, inp_ref, read_ref, s_ref, in_ref, dl_ref, lat_ref, dr_ref, *rest):
+    got_ref = rest[-1]
+    r = row_of(slot, row_ref)
+    lats = []
     for k in range(2):
         at = k * MEM
-        if edge:
-            xs_ref[10 * r + k] = widen(lat_ref[k], dl_ref[at : at + MEM, :HALF], dr_ref[at : at + MEM])
-        else:
-            xs_ref[10 * r + k] = jnp.zeros(xs_ref.shape[1:], F32)
-    empty = jnp.zeros((MEM, s0_ref.shape[1]), F32)
-    per = s0_ref.shape[0] // 4
-    rows = []
-    for res in range(4):
-        rows.append(fl_ref[r, (res - 2) * MEM : (res - 1) * MEM, : 2 * HALF].astype(F32) if res >= 2 else empty)
-        rows.append(s0_ref[res * per : (res + 1) * per].astype(F32))
-        rows.append(fr_ref[r, res * MEM : (res + 1) * MEM].astype(F32) if res < 2 else empty)
-    s_ref[...] = jnp.concatenate(rows, axis=0).astype(BF)
-    in_ref[...] = windows([xs_ref[4 * r + d] for d in range(8)], False)
+        lats.append(widen(lat_ref[k], dl_ref[at : at + MEM, :HALF], dr_ref[at : at + MEM]))
+    got_ref[...] = windows(lats, False)
     bands, cidx, iidx = band_ref[...], cidx_ref[...], iidx_ref[...]
     band = jnp.where(r == 0, bands[0], bands[1])
-    pres = [block_pre(b, band, s_ref, in_ref, cidx, iidx, coup_ref, inp_ref) for b in range(iidx_ref.shape[1])]
-    state = jnp.concatenate([jnp.tanh(p).astype(BF) for p in pres], axis=1)
-    if edge:
-        send_edge(r, state, read_ref, *outs)
-        return
-    outs[0][...] = state
+    parts = []
+    for b in range(iidx_ref.shape[1]):
+        k = of_band(band, iidx, b) - 15 * r
+        used = jnp.logical_and(k >= 0, k < 5)
+        pre = block_pre(b, band, s_ref, in_ref, cidx, iidx, coup_ref, inp_ref, (used, got_ref, block_at(k, got_ref)))
+        parts.append(jnp.tanh(pre).astype(BF))
+    send_edge(r, jnp.concatenate(parts, axis=1), read_ref, *rest[:3])
 
 
 def narrowed(s):
@@ -394,29 +411,26 @@
     padded = vm((12, wide, CHUNK), F32)
     send_out = [bf(2, own_rows, CHUNK + NEAR // 2), bf(2, wide, CHUNK), bf(rows, units)]
 
-    sent, edges, states, far = [None] * slots, [None] * slots, [None] * slots, []
-    for slot in (1, 0):
-        edge = slot < slots
-        operands = [row] + small + weights + [own, ((s0, s1)[slot], VM), (from_left, VM)]
-        if edge:
-            operands.append((from_dleft[slot], VM))
-        operands.append((from_lat[slot if edge else 0], VM))
-        operands.append((from_right, VM))
-        if edge:
-            operands.append((from_dright[slot], VM))
-            operands += [(x, VM) for x in far]
-        got = call(
-            functools.partial(first_kernel, slot, edge, len(far)),
-            send_out if edge else [bf(rows, units)],
-            [VM] * (3 if edge else 1),
-            [padded, vm((rows, units)), vm((rows, 16 * CELL))],
-            operands,
-            flops if edge else 0,
+    first = call(
+        functools.partial(first_kernel, slots),
+        [bf(rows, units), bf(rows, 16 * CELL)] * slots + [bf(rows, units)] * (2 - slots),
+        [VM] * (2 + slots),
+        [padded, vm((rows, units)), vm((rows, 16 * CELL))],
+        [row] + small + weights[:2] + [own, (s0, VM), (s1, VM), (from_left, VM)] + [(x, VM) for x in from_lat] + [(from_right, VM)],
+    )
+    far = list(first[2 * slots :])
+    sent, edges, states = [None] * slots, [None] * slots, [None] * slots
+    for slot in range(slots):
+        known = [(x, VM) for x in first[2 * slot : 2 * slot + 2]]
+        corners = [(x[slot], VM) for x in (from_dleft, from_lat, from_dright)]
+        sent[slot], edges[slot], states[slot] = call(
+            functools.partial(first_edge_kernel, slot),
+            send_out,
+            [VM] * 3,
+            [vm((rows, 4 * CELL))],
+            [row] + small + weights + known + corners,
+            flops,
         )
-        if edge:
-            sent[slot], edges[slot], states[slot] = got
-        else:
-            far = list(got)
 
     for step in range(1, STEPS):
         last = step == STEPS - 1

time: 24.1 us -> 24.1 us (level)
  starting transfers between devices: 11.9 us -> 11.4 us
  waiting for transfers between devices: 1.14 us -> 1.53 us
    ppermute x7, starting transfers between devices: 11.9 us -> 11.4 us  [send(): return lax.ppermute(x, ('lat', 'lon'), pairs)]
    ppermute x7, waiting for transfers between devices: 1.14 us -> 1.53 us  [send(): return lax.ppermute(x, ('lat', 'lon'), pairs)]
where the time goes in v4:
time: 24.1 us; the launch traced here: 24 us
  starting transfers between devices  11.4 us (47%)
  Pallas kernels  9.93 us (41%)
  waiting for transfers between devices  1.53 us (6%)
  between operations  0.81 us (3%)
  local copies, waits for them, and re-layouts  0.27 us (1%)
    ppermute x7, starting transfers between devices, send(): return lax.ppermute(x, ('lat', 'lon'), pairs)  11.4 us
    pallas_call x9, Pallas kernels, call(): pl.pallas_call(kernel, out_shape=out_shape, in_specs=[s for _, s in opera...  9.93 us
    ppermute x7, waiting for transfers between devices, send(): return lax.ppermute(x, ('lat', 'lon'), pairs)  1.53 us
  transfers between devices with their start and end apart: 7, of which 4 were waited for; matrix products, arithmetic and copies ran while one was open for 0% of the time, Pallas kernels for 23%

profile of v4, /device:TPU:0, one launch (start us, length us, event | category | flops | bytes accessed | tf_op | source)
XLA Modules:
  0.0 24.0 jit_solution(13103756079764193582)
XLA Ops:
  0.6 0.0 copy-start.6
  0.6 1.1 %shard_map.95 = (bf16[4,8,1024]{2,1,0:T(8,128)(2,1)S(1)}, bf16[4,8,1024]{2,1,0:T(8,128)(2,1)S(1)}, bf16[8,16,640]{2,1,0:T(8,128)(2,1)S(1)}, bf16[8,1536]{1,0:T(8...) custom-call(s32[1]{0:T(128)} %bitcast.row_ref, bf16[4,8,2560]{2,1,0:T(8,128)(2,1)} %field_hbm.1, ...), custom_call_target="tpu_custom_call" | custom-call | flops 10000000000 | bytes 425988 | tf_op jit(solution)/shard_map/pallas_call | solution.py:336
  1.8 0.0 copy-start.1
  1.8 0.0 copy-start.2
  1.8 0.0 copy-start.3
  1.8 0.0 copy-start.4
  1.8 0.0 copy-start.5
  1.8 0.5 %collective-permute-start = (bf16[4,8,1024]{2,1,0:T(8,128)(2,1)S(1)}, bf16[4,8,1024]{2,1,0:T(8,128)(2,1)S(1)}, u32[]{:S(2)}, u32[]{:S(2)}) collective-permute-start(bf16[4,8,1024]{2,1,0:T(8,128)(2,1)S(1)} %get-tuple-element.24), channel_id=1, source_target_pairs={{0,1},{1,2},{2,3},{3,4},{4,5},{5,6},{6,7},{7,8},{8,9},{9,10},{10,1... | collective-permute-start | bytes 196616 | tf_op jit(solution)/shard_map/ppermute | solution.py:375
  2.3 3.7 %collective-permute-start.1 = (bf16[8,1536]{1,0:T(8,128)(2,1)S(1)}, bf16[8,1536]{1,0:T(8,128)(2,1)S(1)}, u32[]{:S(2)}, u32[]{:S(2)}) collective-permute-start(bf16[8,1536]{1,0:T(8,128)(2,1)S(1)} %get-tuple-element.25), channel_id=1, source_target_pairs={{0,17},{1,18},{2,19},{3,20},{4,21},{5,22},{6,23},{7,24},{8,25},{9,... | collective-permute-start | bytes 73736 | tf_op jit(solution)/shard_map/ppermute | solution.py:375
  6.0 0.5 %collective-permute-start.2 = (bf16[2,16,640]{2,1,0:T(8,128)(2,1)S(1)}, bf16[2,16,640]{2,1,0:T(8,128)(2,1)S(1)}, u32[]{:S(2)}, u32[]{:S(2)}) collective-permute-start(bf16[2,16,640]{2,1,0:T(8,128)(2,1)S(1)} %get-tuple-element.26), channel_id=1, source_target_pairs={{0,16},{1,17},{2,18},{3,19},{4,20},{5,21},{6,22},{7,23},{8,24},{9,... | collective-permute-start | bytes 122888 | tf_op jit(solution)/shard_map/ppermute | solution.py:375
  6.6 2.4 %collective-permute-start.3 = (bf16[4,8,1024]{2,1,0:T(8,128)(2,1)S(1)}, bf16[4,8,1024]{2,1,0:T(8,128)(2,1)S(1)}, u32[]{:S(2)}, u32[]{:S(2)}) collective-permute-start(bf16[4,8,1024]{2,1,0:T(8,128)(2,1)S(1)} %get-tuple-element.27), channel_id=1, source_target_pairs={{0,15},{1,0},{2,1},{3,2},{4,3},{5,4},{6,5},{7,6},{8,7},{9,8},{10,9... | collective-permute-start | bytes 196616 | tf_op jit(solution)/shard_map/ppermute | solution.py:375
  9.0 1.8 %collective-permute-start.4 = (bf16[8,512]{1,0:T(8,128)(2,1)S(1)}, bf16[8,512]{1,0:T(8,128)(2,1)S(1)}, u32[]{:S(2)}, u32[]{:S(2)}) collective-permute-start(bf16[8,512]{1,0:T(8,128)(2,1)S(1)} %get-tuple-element.30), channel_id=1, source_target_pairs={{0,31},{1,16},{2,17},{3,18},{4,19},{5,20},{6,21},{7,22},{8,23},{9,... | collective-permute-start | bytes 24584 | tf_op jit(solution)/shard_map/ppermute | solution.py:375
  10.8 0.2 collective-permute-done.1.rest_1_.dl_ref
  11.0 0.0 collective-permute-done.rest_0_.fl_ref
  11.0 0.0 copy-done.6
  11.0 0.0 collective-permute-done.2.rest_0_.lat_ref
  11.1 0.0 copy-start
  11.1 0.0 collective-permute-done.3.rest_1_
  11.1 0.0 copy-done.1
  11.1 0.0 copy-done.2
  11.2 0.9 %shard_map.98 = (bf16[96,1024]{1,0:T(8,128)(2,1)S(1)}, bf16[96,2560]{1,0:T(8,128)(2,1)S(1)}, bf16[96,1024]{1,0:T(8,128)(2,1)S(1)}) custom-call(s32[1]{0:T(128)} %bitcast.row_ref, s32[2]{0:T(128)S(1)} %copy-done.5, s32[2,2,8]{2,1,0:T(2,128)S(1)} %bitcast.8, s32[2,8]{1,0:T(2,128)S(1)} %copy-done.3, bf16[2,2048,128]{2,1,0:T(8,128)(2,1)S(1)} %copy-done.2, ...), custom_call_target="tpu_custom_call" | custom-call | bytes 2171084 | tf_op jit(solution)/shard_map/pallas_call | solution.py:336
  12.0 0.1 collective-permute-done.4.dr_ref
  12.2 0.2 copy-done
  12.4 0.9 %shard_map.99 = (bf16[2,16,768]{2,1,0:T(8,128)(2,1)S(1)}, bf16[2,24,640]{2,1,0:T(8,128)(2,1)S(1)}, bf16[96,1024]{1,0:T(8,128)(2,1)S(1)}) custom-call(s32[1]{0:T(128)} %bitcast.row_ref, s32[2]{0:T(128)S(1)} %copy-done.5, s32[2,2,8]{2,1,0:T(2,128)S(1)} %bitcast.9, s32[2,8]{1,0:T(2,128)S(1)} %copy-done.3, bf16[2,2048,128]{2,1,0:T(8,128)(2,1)S(1)} %copy-done.2, ...), custom_call_target="tpu_custom_call" | custom-call | flops 201326592 | bytes 3645644 | tf_op jit(solution)/shard_map/pallas_call | solution.py:336
  13.3 1.2 %collective-permute-start.5 = (bf16[2,16,768]{2,1,0:T(8,128)(2,1)S(1)}, bf16[2,16,768]{2,1,0:T(8,128)(2,1)S(1)}, u32[]{:S(2)}, u32[]{:S(2)}) collective-permute-start(bf16[2,16,768]{2,1,0:T(8,128)(2,1)S(1)} %get-tuple-element.35), channel_id=1, source_target_pairs={{0,16},{1,17},{2,18},{3,19},{4,20},{5,21},{6,22},{7,23},{8,24},{9,... | collective-permute-start | bytes 147464 | tf_op jit(solution)/shard_map/ppermute | solution.py:375
  14.5 2.1 %shard_map.100 = (f32[96,1024]{1,0:T(8,128)S(1)}, bf16[4,24,640]{2,1,0:T(8,128)(2,1)S(1)}, bf16[96,1024]{1,0:T(8,128)(2,1)S(1)}) custom-call(s32[1]{0:T(128)} %bitcast.row_ref, s32[2]{0:T(128)S(1)} %copy-done.5, s32[2,2,8]{2,1,0:T(2,128)S(1)} %bitcast.10, s32[2,8]{1,0:T(2,128)S(1)} %copy-done.3, bf16[2,2048,128]{2,1,0:T(8,128)(2,1)S(1)} %copy-done.2, ...), custom_call_target="tpu_custom_call" | custom-call | flops 402653184 | bytes 3338444 | tf_op jit(solution)/shard_map/pallas_call | solution.py:336
  16.6 0.8 %collective-permute-done.5.got_ref = bf16[2,16,768]{2,1,0:T(8,128)(2,1)S(1)} collective-permute-done((bf16[2,16,768]{2,1,0:T(8,128)(2,1)S(1)}, bf16[2,16,768]{2,1,0:T(8,128)(2,1)S(1)}, u32[]{:S(2)}, u32[]{:S(2)}) %collective-permute-start.5) | collective-permute-done | bytes 49184 | tf_op jit(solution)/shard_map/ppermute | solution.py:375
  17.5 0.7 %shard_map.101 = (bf16[2,16,768]{2,1,0:T(8,128)(2,1)S(1)}, bf16[2,24,640]{2,1,0:T(8,128)(2,1)S(1)}, bf16[96,1024]{1,0:T(8,128)(2,1)S(1)}) custom-call(s32[1]{0:T(128)} %bitcast.row_ref, s32[2]{0:T(128)S(1)} %copy-done.5, s32[2,8]{1,0:T(2,128)S(1)} %copy-done.3, bf16[2,1024,128]{2,1,0:T(8,128)(2,1)S(1)} %copy-done.1, bf16[640,1024]{1,0:T(8,128)(2,1)S(1)} %bitcast.5, ...), custom_call_target="tpu_custom_call" | custom-call | flops 201326592 | bytes 2277452 | tf_op jit(solution)/shard_map/pallas_call | solution.py:336
  18.2 1.2 %collective-permute-start.6 = (bf16[2,16,768]{2,1,0:T(8,128)(2,1)S(1)}, bf16[2,16,768]{2,1,0:T(8,128)(2,1)S(1)}, u32[]{:S(2)}, u32[]{:S(2)}) collective-permute-start(bf16[2,16,768]{2,1,0:T(8,128)(2,1)S(1)} %get-tuple-element.41), channel_id=1, source_target_pairs={{0,16},{1,17},{2,18},{3,19},{4,20},{5,21},{6,22},{7,23},{8,24},{9,... | collective-permute-start | bytes 147464 | tf_op jit(solution)/shard_map/ppermute | solution.py:375
  19.4 2.6 %shard_map.102 = (f32[64,1024]{1,0:T(8,128)S(1)}, bf16[4,16,640]{2,1,0:T(8,128)(2,1)S(1)}, bf16[2,16,4,1024]{3,2,1,0:T(4,128)(2,1)}) custom-call(s32[1]{0:T(128)} %bitcast.row_ref, s32[2]{0:T(128)S(1)} %copy-done.5, s32[2,2,8]{2,1,0:T(2,128)S(1)} %bitcast.11, s32[2,8]{1,0:T(2,128)S(1)} %copy-done.3, bf16[2,2048,128]{2,1,0:T(8,128)(2,1)S(1)} %copy-done.2, ...), custom_call_target="tpu_custom_call" | custom-call | flops 402653184 | bytes 3461324 | tf_op jit(solution)/shard_map/pallas_call | solution.py:336
  22.0 0.4 %collective-permute-done.6.got_ref = bf16[2,16,768]{2,1,0:T(8,128)(2,1)S(1)} collective-permute-done((bf16[2,16,768]{2,1,0:T(8,128)(2,1)S(1)}, bf16[2,16,768]{2,1,0:T(8,128)(2,1)S(1)}, u32[]{:S(2)}, u32[]{:S(2)}) %collective-permute-start.6) | collective-permute-done | bytes 49184 | tf_op jit(solution)/shard_map/ppermute | solution.py:375
  22.4 1.6 %shard_map.103 = (bf16[4,8,2560]{2,1,0:T(8,128)(2,1)}, bf16[2,16,4,1024]{3,2,1,0:T(4,128)(2,1)}) custom-call(s32[1]{0:T(128)} %bitcast.row_ref, s32[2]{0:T(128)S(1)} %copy-done.5, s32[2,8]{1,0:T(2,128)S(1)} %copy-done.3, bf16[2,1024,128]{2,1,0:T(8,128)(2,1)S(1)} %copy-done.1, bf16[640,1024]{1,0:T(8,128)(2,1)S(1)} %bitcast.7, ...), custom_call_target="tpu_custom_call", output_to_operand_aliasing={{1}: (8, {})} | custom-call | flops 201326592 | bytes 2490444 | tf_op jit(solution)/shard_map/pallas_call | solution.py:336
  (5 shorter events, 0.1 us)
Async XLA Ops:
  0.6 10.4 %copy-start.6 = (bf16[2,16,4,1024]{3,2,1,0:T(4,128)(2,1)S(1)}, bf16[2,16,4,1024]{3,2,1,0:T(4,128)(2,1)}, u32[]{:S(2)}) copy-start(bf16[2,16,4,1024]{3,2,1,0:T(4,128)(2,1)} %state_ref.3) | copy-start | bytes 786436
  1.8 9.4 %copy-start.1 = (bf16[2,1024,128]{2,1,0:T(8,128)(2,1)S(1)}, bf16[2,1024,128]{2,1,0:T(8,128)(2,1)}, u32[]{:S(2)}) copy-start(bf16[2,1024,128]{2,1,0:T(8,128)(2,1)} %inp_ref.11) | copy-start | bytes 1572868
  1.8 9.4 %copy-start.2 = (bf16[2,2048,128]{2,1,0:T(8,128)(2,1)S(1)}, bf16[2,2048,128]{2,1,0:T(8,128)(2,1)}, u32[]{:S(2)}) copy-start(bf16[2,2048,128]{2,1,0:T(8,128)(2,1)} %coup_ref.7) | copy-start | bytes 3145732
  1.8 9.4 %copy-start.3 = (s32[2,8]{1,0:T(2,128)S(1)}, s32[2,8]{1,0:T(2,128)}, u32[]{:S(2)}) copy-start(s32[2,8]{1,0:T(2,128)} %iidx_ref.11) | copy-start | bytes 196
  1.8 9.4 %copy-start.4 = (s32[2,8,2]{1,2,0:T(2,128)S(1)}, s32[2,8,2]{1,2,0:T(2,128)}, u32[]{:S(2)}) copy-start(s32[2,8,2]{1,2,0:T(2,128)} %param.11) | copy-start | bytes 388
  1.8 9.4 %copy-start.5 = (s32[2]{0:T(128)S(1)}, s32[2]{0:T(128)}, u32[]{:S(2)}) copy-start(s32[2]{0:T(128)} %band_ref.11) | copy-start | bytes 28
  1.8 9.2 %collective-permute-start = (bf16[4,8,1024]{2,1,0:T(8,128)(2,1)S(1)}, bf16[4,8,1024]{2,1,0:T(8,128)(2,1)S(1)}, u32[]{:S(2)}, u32[]{:S(2)}) collective-permute-start(bf16[4,8,1024]{2,1,0:T(8,128)(2,1)S(1)} %get-tuple-element.24), channel_id=1, source_target_pairs={{0,1},{1,2},{2,3},{3,4},{4,5},{5,6},{6,7},{7,8},{8,9},{9,10},{10,1... | collective-permute-start | bytes 196616 | tf_op jit(solution)/shard_map/ppermute | solution.py:375
  2.3 8.7 %collective-permute-start.1 = (bf16[8,1536]{1,0:T(8,128)(2,1)S(1)}, bf16[8,1536]{1,0:T(8,128)(2,1)S(1)}, u32[]{:S(2)}, u32[]{:S(2)}) collective-permute-start(bf16[8,1536]{1,0:T(8,128)(2,1)S(1)} %get-tuple-element.25), channel_id=1, source_target_pairs={{0,17},{1,18},{2,19},{3,20},{4,21},{5,22},{6,23},{7,24},{8,25},{9,... | collective-permute-start | bytes 73736 | tf_op jit(solution)/shard_map/ppermute | solution.py:375
  6.0 5.0 %collective-permute-start.2 = (bf16[2,16,640]{2,1,0:T(8,128)(2,1)S(1)}, bf16[2,16,640]{2,1,0:T(8,128)(2,1)S(1)}, u32[]{:S(2)}, u32[]{:S(2)}) collective-permute-start(bf16[2,16,640]{2,1,0:T(8,128)(2,1)S(1)} %get-tuple-element.26), channel_id=1, source_target_pairs={{0,16},{1,17},{2,18},{3,19},{4,20},{5,21},{6,22},{7,23},{8,24},{9,... | collective-permute-start | bytes 122888 | tf_op jit(solution)/shard_map/ppermute | solution.py:375
  6.6 4.5 %collective-permute-start.3 = (bf16[4,8,1024]{2,1,0:T(8,128)(2,1)S(1)}, bf16[4,8,1024]{2,1,0:T(8,128)(2,1)S(1)}, u32[]{:S(2)}, u32[]{:S(2)}) collective-permute-start(bf16[4,8,1024]{2,1,0:T(8,128)(2,1)S(1)} %get-tuple-element.27), channel_id=1, source_target_pairs={{0,15},{1,0},{2,1},{3,2},{4,3},{5,4},{6,5},{7,6},{8,7},{9,8},{10,9... | collective-permute-start | bytes 196616 | tf_op jit(solution)/shard_map/ppermute | solution.py:375
  9.0 3.2 %collective-permute-start.4 = (bf16[8,512]{1,0:T(8,128)(2,1)S(1)}, bf16[8,512]{1,0:T(8,128)(2,1)S(1)}, u32[]{:S(2)}, u32[]{:S(2)}) collective-permute-start(bf16[8,512]{1,0:T(8,128)(2,1)S(1)} %get-tuple-element.30), channel_id=1, source_target_pairs={{0,31},{1,16},{2,17},{3,18},{4,19},{5,20},{6,21},{7,22},{8,23},{9,... | collective-permute-start | bytes 24584 | tf_op jit(solution)/shard_map/ppermute | solution.py:375
  11.1 1.3 %copy-start = (bf16[1,640,1024]{2,1,0:T(8,128)(2,1)S(1)}, bf16[1,640,1024]{2,1,0:T(8,128)(2,1)}, u32[]{:S(2)}) copy-start(bf16[1,640,1024]{2,1,0:T(8,128)(2,1)} %param.14) | copy-start | bytes 3932164
  13.3 4.2 %collective-permute-start.5 = (bf16[2,16,768]{2,1,0:T(8,128)(2,1)S(1)}, bf16[2,16,768]{2,1,0:T(8,128)(2,1)S(1)}, u32[]{:S(2)}, u32[]{:S(2)}) collective-permute-start(bf16[2,16,768]{2,1,0:T(8,128)(2,1)S(1)} %get-tuple-element.35), channel_id=1, source_target_pairs={{0,16},{1,17},{2,18},{3,19},{4,20},{5,21},{6,22},{7,23},{8,24},{9,... | collective-permute-start | bytes 147464 | tf_op jit(solution)/shard_map/ppermute | solution.py:375
  18.2 4.2 %collective-permute-start.6 = (bf16[2,16,768]{2,1,0:T(8,128)(2,1)S(1)}, bf16[2,16,768]{2,1,0:T(8,128)(2,1)S(1)}, u32[]{:S(2)}, u32[]{:S(2)}) collective-permute-start(bf16[2,16,768]{2,1,0:T(8,128)(2,1)S(1)} %get-tuple-element.41), channel_id=1, source_target_pairs={{0,16},{1,17},{2,18},{3,19},{4,20},{5,21},{6,22},{7,23},{8,24},{9,... | collective-permute-start | bytes 147464 | tf_op jit(solution)/shard_map/ppermute | solution.py:375

commit v5 on v4

--- a/solution.py
+++ b/solution.py
@@ -155,7 +155,7 @@
     return jnp.concatenate([left, own.astype(F32), right], axis=0)
 
 
-def first_kernel(slots, row_ref, band_ref, cidx_ref, iidx_ref, coup_ref, inp_ref, own_ref, s0_ref, s1_ref, fl_ref, *rest):
+def first_kernel(slots, row_ref, band_ref, cidx_ref, iidx_ref, coup_ref, inp_ref, _, own_ref, s0_ref, s1_ref, fl_ref, *rest):
     fr_ref = rest[slots]
     outs = rest[slots + 1 : -3]
     xs_ref, s_ref, in_ref = rest[-3:]
@@ -308,8 +308,8 @@
         lats_ref, states_hbm, stage_ref, sem = rest[:4]
     else:
         other_ref, _, field_hbm, states_hbm, stage_ref, sem, field_ref, field_sem = rest[:8]
+    pred = lax.dot_general(state, read_ref[...], NT, preferred_element_type=F32)
     copy = put_states(r, state, stage_ref, states_hbm, sem)
-    pred = lax.dot_general(state, read_ref[...], NT, preferred_element_type=F32)
     mine = [latitude(pred, d) for d in range(4)]
     if not final:
         for d in range(4):
@@ -416,7 +416,7 @@
         [bf(rows, units), bf(rows, 16 * CELL)] * slots + [bf(rows, units)] * (2 - slots),
         [VM] * (2 + slots),
         [padded, vm((rows, units)), vm((rows, 16 * CELL))],
-        [row] + small + weights[:2] + [own, (s0, VM), (s1, VM), (from_left, VM)] + [(x, VM) for x in from_lat] + [(from_right, VM)],
+        [row] + small + weights + [own, (s0, VM), (s1, VM), (from_left, VM)] + [(x, VM) for x in from_lat] + [(from_right, VM)],
     )
     far = list(first[2 * slots :])
     sent, edges, states = [None] * slots, [None] * slots, [None] * slots

time: 24.1 us -> 24 us (level)
  starting transfers between devices: 11.4 us -> 11.9 us
  waiting for transfers between devices: 1.53 us -> 1.09 us
    ppermute x7, starting transfers between devices: 11.4 us -> 11.9 us  [send(): return lax.ppermute(x, ('lat', 'lon'), pairs)]
    ppermute x7, waiting for transfers between devices: 1.53 us -> 1.09 us  [send(): return lax.ppermute(x, ('lat', 'lon'), pairs)]
  transfers between devices with their start and end apart: 7 -> 7, of which waited for: 4 -> 4; matrix products, arithmetic and copies ran while one was open for 0% -> 0% of each run, Pallas kernels for 23% -> 24%
where the time goes in v5:
time: 24 us; the launch traced here: 23.8 us
  starting transfers between devices  11.9 us (50%)
  Pallas kernels  9.98 us (42%)
  waiting for transfers between devices  1.09 us (5%)
  between operations  0.82 us (3%)
    ppermute x7, starting transfers between devices, send(): return lax.ppermute(x, ('lat', 'lon'), pairs)  11.9 us
    pallas_call x9, Pallas kernels, call(): pl.pallas_call(kernel, out_shape=out_shape, in_specs=[s for _, s in opera...  9.98 us
    ppermute x7, waiting for transfers between devices, send(): return lax.ppermute(x, ('lat', 'lon'), pairs)  1.09 us
  transfers between devices with their start and end apart: 7, of which 4 were waited for; matrix products, arithmetic and copies ran while one was open for 0% of the time, Pallas kernels for 24%

profile of v5, /device:TPU:0, one launch (start us, length us, event | category | flops | bytes accessed | tf_op | source)
XLA Modules:
  0.0 23.8 jit_solution(3859704363024356273)
XLA Ops:
  0.6 0.0 copy-start.6
  0.6 0.0 copy-start.2
  0.7 1.2 %shard_map.95 = (bf16[4,8,1024]{2,1,0:T(8,128)(2,1)S(1)}, bf16[4,8,1024]{2,1,0:T(8,128)(2,1)S(1)}, bf16[8,16,640]{2,1,0:T(8,128)(2,1)S(1)}, bf16[8,1536]{1,0:T(8...) custom-call(s32[1]{0:T(128)} %bitcast.row_ref, bf16[4,8,2560]{2,1,0:T(8,128)(2,1)} %field_hbm.1, ...), custom_call_target="tpu_custom_call" | custom-call | flops 10000000000 | bytes 425988 | tf_op jit(solution)/shard_map/pallas_call | solution.py:336
  1.8 0.0 copy-start
  1.8 0.0 copy-start.1
  1.8 0.0 copy-start.3
  1.9 0.0 copy-start.4
  1.9 0.0 copy-start.5
  1.9 0.5 %collective-permute-start = (bf16[4,8,1024]{2,1,0:T(8,128)(2,1)S(1)}, bf16[4,8,1024]{2,1,0:T(8,128)(2,1)S(1)}, u32[]{:S(2)}, u32[]{:S(2)}) collective-permute-start(bf16[4,8,1024]{2,1,0:T(8,128)(2,1)S(1)} %get-tuple-element.24), channel_id=1, source_target_pairs={{0,1},{1,2},{2,3},{3,4},{4,5},{5,6},{6,7},{7,8},{8,9},{9,10},{10,1... | collective-permute-start | bytes 196616 | tf_op jit(solution)/shard_map/ppermute | solution.py:375
  2.4 3.7 %collective-permute-start.1 = (bf16[8,1536]{1,0:T(8,128)(2,1)S(1)}, bf16[8,1536]{1,0:T(8,128)(2,1)S(1)}, u32[]{:S(2)}, u32[]{:S(2)}) collective-permute-start(bf16[8,1536]{1,0:T(8,128)(2,1)S(1)} %get-tuple-element.25), channel_id=1, source_target_pairs={{0,17},{1,18},{2,19},{3,20},{4,21},{5,22},{6,23},{7,24},{8,25},{9,... | collective-permute-start | bytes 73736 | tf_op jit(solution)/shard_map/ppermute | solution.py:375
  6.1 0.5 %collective-permute-start.2 = (bf16[2,16,640]{2,1,0:T(8,128)(2,1)S(1)}, bf16[2,16,640]{2,1,0:T(8,128)(2,1)S(1)}, u32[]{:S(2)}, u32[]{:S(2)}) collective-permute-start(bf16[2,16,640]{2,1,0:T(8,128)(2,1)S(1)} %get-tuple-element.26), channel_id=1, source_target_pairs={{0,16},{1,17},{2,18},{3,19},{4,20},{5,21},{6,22},{7,23},{8,24},{9,... | collective-permute-start | bytes 122888 | tf_op jit(solution)/shard_map/ppermute | solution.py:375
  6.6 2.4 %collective-permute-start.3 = (bf16[4,8,1024]{2,1,0:T(8,128)(2,1)S(1)}, bf16[4,8,1024]{2,1,0:T(8,128)(2,1)S(1)}, u32[]{:S(2)}, u32[]{:S(2)}) collective-permute-start(bf16[4,8,1024]{2,1,0:T(8,128)(2,1)S(1)} %get-tuple-element.27), channel_id=1, source_target_pairs={{0,15},{1,0},{2,1},{3,2},{4,3},{5,4},{6,5},{7,6},{8,7},{9,8},{10,9... | collective-permute-start | bytes 196616 | tf_op jit(solution)/shard_map/ppermute | solution.py:375
  9.1 1.8 %collective-permute-start.4 = (bf16[8,512]{1,0:T(8,128)(2,1)S(1)}, bf16[8,512]{1,0:T(8,128)(2,1)S(1)}, u32[]{:S(2)}, u32[]{:S(2)}) collective-permute-start(bf16[8,512]{1,0:T(8,128)(2,1)S(1)} %get-tuple-element.30), channel_id=1, source_target_pairs={{0,31},{1,16},{2,17},{3,18},{4,19},{5,20},{6,21},{7,22},{8,23},{9,... | collective-permute-start | bytes 24584 | tf_op jit(solution)/shard_map/ppermute | solution.py:375
  10.9 0.2 collective-permute-done.1.rest_1_.dl_ref
  11.1 0.0 collective-permute-done.rest_0_.fl_ref
  11.1 0.0 copy-done.6
  11.1 0.0 collective-permute-done.2.rest_0_.lat_ref
  11.2 0.0 collective-permute-done.3.rest_1_
  11.2 0.0 copy-done.2
  11.2 0.0 copy-done
  11.2 0.0 copy-done.1
  11.2 0.9 %shard_map.98 = (bf16[96,1024]{1,0:T(8,128)(2,1)S(1)}, bf16[96,2560]{1,0:T(8,128)(2,1)S(1)}, bf16[96,1024]{1,0:T(8,128)(2,1)S(1)}) custom-call(s32[1]{0:T(128)} %bitcast.row_ref, s32[2]{0:T(128)S(1)} %copy-done.5, s32[2,2,8]{2,1,0:T(2,128)S(1)} %bitcast.9, s32[2,8]{1,0:T(2,128)S(1)} %copy-done.3, bf16[2,2048,128]{2,1,0:T(8,128)(2,1)S(1)} %copy-done.2, ...), custom_call_target="tpu_custom_call" | custom-call | bytes 3481804 | tf_op jit(solution)/shard_map/pallas_call | solution.py:336
  12.1 0.1 collective-permute-done.4.dr_ref
  12.3 0.9 %shard_map.99 = (bf16[2,16,768]{2,1,0:T(8,128)(2,1)S(1)}, bf16[2,24,640]{2,1,0:T(8,128)(2,1)S(1)}, bf16[96,1024]{1,0:T(8,128)(2,1)S(1)}) custom-call(s32[1]{0:T(128)} %bitcast.row_ref, s32[2]{0:T(128)S(1)} %copy-done.5, s32[2,2,8]{2,1,0:T(2,128)S(1)} %bitcast.10, s32[2,8]{1,0:T(2,128)S(1)} %copy-done.3, bf16[2,2048,128]{2,1,0:T(8,128)(2,1)S(1)} %copy-done.2, ...), custom_call_target="tpu_custom_call" | custom-call | flops 201326592 | bytes 3645644 | tf_op jit(solution)/shard_map/pallas_call | solution.py:336
  13.2 1.4 %collective-permute-start.5 = (bf16[2,16,768]{2,1,0:T(8,128)(2,1)S(1)}, bf16[2,16,768]{2,1,0:T(8,128)(2,1)S(1)}, u32[]{:S(2)}, u32[]{:S(2)}) collective-permute-start(bf16[2,16,768]{2,1,0:T(8,128)(2,1)S(1)} %get-tuple-element.35), channel_id=1, source_target_pairs={{0,16},{1,17},{2,18},{3,19},{4,20},{5,21},{6,22},{7,23},{8,24},{9,... | collective-permute-start | bytes 147464 | tf_op jit(solution)/shard_map/ppermute | solution.py:375
  14.6 2.1 %shard_map.100 = (f32[96,1024]{1,0:T(8,128)S(1)}, bf16[4,24,640]{2,1,0:T(8,128)(2,1)S(1)}, bf16[96,1024]{1,0:T(8,128)(2,1)S(1)}) custom-call(s32[1]{0:T(128)} %bitcast.row_ref, s32[2]{0:T(128)S(1)} %copy-done.5, s32[2,2,8]{2,1,0:T(2,128)S(1)} %bitcast.11, s32[2,8]{1,0:T(2,128)S(1)} %copy-done.3, bf16[2,2048,128]{2,1,0:T(8,128)(2,1)S(1)} %copy-done.2, ...), custom_call_target="tpu_custom_call" | custom-call | flops 402653184 | bytes 3338444 | tf_op jit(solution)/shard_map/pallas_call | solution.py:336
  16.7 0.6 %collective-permute-done.5.got_ref = bf16[2,16,768]{2,1,0:T(8,128)(2,1)S(1)} collective-permute-done((bf16[2,16,768]{2,1,0:T(8,128)(2,1)S(1)}, bf16[2,16,768]{2,1,0:T(8,128)(2,1)S(1)}, u32[]{:S(2)}, u32[]{:S(2)}) %collective-permute-start.5) | collective-permute-done | bytes 49184 | tf_op jit(solution)/shard_map/ppermute | solution.py:375
  17.3 0.7 %shard_map.101 = (bf16[2,16,768]{2,1,0:T(8,128)(2,1)S(1)}, bf16[2,24,640]{2,1,0:T(8,128)(2,1)S(1)}, bf16[96,1024]{1,0:T(8,128)(2,1)S(1)}) custom-call(s32[1]{0:T(128)} %bitcast.row_ref, s32[2]{0:T(128)S(1)} %copy-done.5, s32[2,8]{1,0:T(2,128)S(1)} %copy-done.3, bf16[2,1024,128]{2,1,0:T(8,128)(2,1)S(1)} %copy-done.1, bf16[640,1024]{1,0:T(8,128)(2,1)S(1)} %bitcast.6, ...), custom_call_target="tpu_custom_call" | custom-call | flops 201326592 | bytes 2277452 | tf_op jit(solution)/shard_map/pallas_call | solution.py:336
  18.0 1.4 %collective-permute-start.6 = (bf16[2,16,768]{2,1,0:T(8,128)(2,1)S(1)}, bf16[2,16,768]{2,1,0:T(8,128)(2,1)S(1)}, u32[]{:S(2)}, u32[]{:S(2)}) collective-permute-start(bf16[2,16,768]{2,1,0:T(8,128)(2,1)S(1)} %get-tuple-element.41), channel_id=1, source_target_pairs={{0,16},{1,17},{2,18},{3,19},{4,20},{5,21},{6,22},{7,23},{8,24},{9,... | collective-permute-start | bytes 147464 | tf_op jit(solution)/shard_map/ppermute | solution.py:375
  19.5 2.6 %shard_map.102 = (f32[64,1024]{1,0:T(8,128)S(1)}, bf16[4,16,640]{2,1,0:T(8,128)(2,1)S(1)}, bf16[2,16,4,1024]{3,2,1,0:T(4,128)(2,1)}) custom-call(s32[1]{0:T(128)} %bitcast.row_ref, s32[2]{0:T(128)S(1)} %copy-done.5, s32[2,2,8]{2,1,0:T(2,128)S(1)} %bitcast.12, s32[2,8]{1,0:T(2,128)S(1)} %copy-done.3, bf16[2,2048,128]{2,1,0:T(8,128)(2,1)S(1)} %copy-done.2, ...), custom_call_target="tpu_custom_call" | custom-call | flops 402653184 | bytes 3461324 | tf_op jit(solution)/shard_map/pallas_call | solution.py:336
  22.0 0.2 collective-permute-done.6.got_ref
  22.2 1.6 %shard_map.103 = (bf16[4,8,2560]{2,1,0:T(8,128)(2,1)}, bf16[2,16,4,1024]{3,2,1,0:T(4,128)(2,1)}) custom-call(s32[1]{0:T(128)} %bitcast.row_ref, s32[2]{0:T(128)S(1)} %copy-done.5, s32[2,8]{1,0:T(2,128)S(1)} %copy-done.3, bf16[2,1024,128]{2,1,0:T(8,128)(2,1)S(1)} %copy-done.1, bf16[640,1024]{1,0:T(8,128)(2,1)S(1)} %bitcast.8, ...), custom_call_target="tpu_custom_call", output_to_operand_aliasing={{1}: (8, {})} | custom-call | flops 201326592 | bytes 2490444 | tf_op jit(solution)/shard_map/pallas_call | solution.py:336
  (5 shorter events, 0.1 us)
Async XLA Ops:
  0.6 10.4 %copy-start.6 = (bf16[2,16,4,1024]{3,2,1,0:T(4,128)(2,1)S(1)}, bf16[2,16,4,1024]{3,2,1,0:T(4,128)(2,1)}, u32[]{:S(2)}) copy-start(bf16[2,16,4,1024]{3,2,1,0:T(4,128)(2,1)} %state_ref.3) | copy-start | bytes 786436
  0.6 10.5 %copy-start.2 = (bf16[2,2048,128]{2,1,0:T(8,128)(2,1)S(1)}, bf16[2,2048,128]{2,1,0:T(8,128)(2,1)}, u32[]{:S(2)}) copy-start(bf16[2,2048,128]{2,1,0:T(8,128)(2,1)} %coup_ref.7) | copy-start | bytes 3145732
  1.8 9.4 %copy-start = (bf16[1,640,1024]{2,1,0:T(8,128)(2,1)S(1)}, bf16[1,640,1024]{2,1,0:T(8,128)(2,1)}, u32[]{:S(2)}) copy-start(bf16[1,640,1024]{2,1,0:T(8,128)(2,1)} %param.14) | copy-start | bytes 3932164
  1.8 9.4 %copy-start.1 = (bf16[2,1024,128]{2,1,0:T(8,128)(2,1)S(1)}, bf16[2,1024,128]{2,1,0:T(8,128)(2,1)}, u32[]{:S(2)}) copy-start(bf16[2,1024,128]{2,1,0:T(8,128)(2,1)} %inp_ref.11) | copy-start | bytes 1572868
  1.8 9.4 %copy-start.3 = (s32[2,8]{1,0:T(2,128)S(1)}, s32[2,8]{1,0:T(2,128)}, u32[]{:S(2)}) copy-start(s32[2,8]{1,0:T(2,128)} %iidx_ref.11) | copy-start | bytes 196
  1.9 9.4 %copy-start.4 = (s32[2,8,2]{1,2,0:T(2,128)S(1)}, s32[2,8,2]{1,2,0:T(2,128)}, u32[]{:S(2)}) copy-start(s32[2,8,2]{1,2,0:T(2,128)} %param.11) | copy-start | bytes 388
  1.9 9.4 %copy-start.5 = (s32[2]{0:T(128)S(1)}, s32[2]{0:T(128)}, u32[]{:S(2)}) copy-start(s32[2]{0:T(128)} %band_ref.11) | copy-start | bytes 28
  1.9 9.2 %collective-permute-start = (bf16[4,8,1024]{2,1,0:T(8,128)(2,1)S(1)}, bf16[4,8,1024]{2,1,0:T(8,128)(2,1)S(1)}, u32[]{:S(2)}, u32[]{:S(2)}) collective-permute-start(bf16[4,8,1024]{2,1,0:T(8,128)(2,1)S(1)} %get-tuple-element.24), channel_id=1, source_target_pairs={{0,1},{1,2},{2,3},{3,4},{4,5},{5,6},{6,7},{7,8},{8,9},{9,10},{10,1... | collective-permute-start | bytes 196616 | tf_op jit(solution)/shard_map/ppermute | solution.py:375
  2.4 8.7 %collective-permute-start.1 = (bf16[8,1536]{1,0:T(8,128)(2,1)S(1)}, bf16[8,1536]{1,0:T(8,128)(2,1)S(1)}, u32[]{:S(2)}, u32[]{:S(2)}) collective-permute-start(bf16[8,1536]{1,0:T(8,128)(2,1)S(1)} %get-tuple-element.25), channel_id=1, source_target_pairs={{0,17},{1,18},{2,19},{3,20},{4,21},{5,22},{6,23},{7,24},{8,25},{9,... | collective-permute-start | bytes 73736 | tf_op jit(solution)/shard_map/ppermute | solution.py:375
  6.1 5.0 %collective-permute-start.2 = (bf16[2,16,640]{2,1,0:T(8,128)(2,1)S(1)}, bf16[2,16,640]{2,1,0:T(8,128)(2,1)S(1)}, u32[]{:S(2)}, u32[]{:S(2)}) collective-permute-start(bf16[2,16,640]{2,1,0:T(8,128)(2,1)S(1)} %get-tuple-element.26), channel_id=1, source_target_pairs={{0,16},{1,17},{2,18},{3,19},{4,20},{5,21},{6,22},{7,23},{8,24},{9,... | collective-permute-start | bytes 122888 | tf_op jit(solution)/shard_map/ppermute | solution.py:375
  6.6 4.5 %collective-permute-start.3 = (bf16[4,8,1024]{2,1,0:T(8,128)(2,1)S(1)}, bf16[4,8,1024]{2,1,0:T(8,128)(2,1)S(1)}, u32[]{:S(2)}, u32[]{:S(2)}) collective-permute-start(bf16[4,8,1024]{2,1,0:T(8,128)(2,1)S(1)} %get-tuple-element.27), channel_id=1, source_target_pairs={{0,15},{1,0},{2,1},{3,2},{4,3},{5,4},{6,5},{7,6},{8,7},{9,8},{10,9... | collective-permute-start | bytes 196616 | tf_op jit(solution)/shard_map/ppermute | solution.py:375
  9.1 3.2 %collective-permute-start.4 = (bf16[8,512]{1,0:T(8,128)(2,1)S(1)}, bf16[8,512]{1,0:T(8,128)(2,1)S(1)}, u32[]{:S(2)}, u32[]{:S(2)}) collective-permute-start(bf16[8,512]{1,0:T(8,128)(2,1)S(1)} %get-tuple-element.30), channel_id=1, source_target_pairs={{0,31},{1,16},{2,17},{3,18},{4,19},{5,20},{6,21},{7,22},{8,23},{9,... | collective-permute-start | bytes 24584 | tf_op jit(solution)/shard_map/ppermute | solution.py:375
  13.2 4.2 %collective-permute-start.5 = (bf16[2,16,768]{2,1,0:T(8,128)(2,1)S(1)}, bf16[2,16,768]{2,1,0:T(8,128)(2,1)S(1)}, u32[]{:S(2)}, u32[]{:S(2)}) collective-permute-start(bf16[2,16,768]{2,1,0:T(8,128)(2,1)S(1)} %get-tuple-element.35), channel_id=1, source_target_pairs={{0,16},{1,17},{2,18},{3,19},{4,20},{5,21},{6,22},{7,23},{8,24},{9,... | collective-permute-start | bytes 147464 | tf_op jit(solution)/shard_map/ppermute | solution.py:375
  18.0 4.2 %collective-permute-start.6 = (bf16[2,16,768]{2,1,0:T(8,128)(2,1)S(1)}, bf16[2,16,768]{2,1,0:T(8,128)(2,1)S(1)}, u32[]{:S(2)}, u32[]{:S(2)}) collective-permute-start(bf16[2,16,768]{2,1,0:T(8,128)(2,1)S(1)} %get-tuple-element.41), channel_id=1, source_target_pairs={{0,16},{1,17},{2,18},{3,19},{4,20},{5,21},{6,22},{7,23},{8,24},{9,... | collective-permute-start | bytes 147464 | tf_op jit(solution)/shard_map/ppermute | solution.py:375

commit v6 on v5

--- a/solution.py
+++ b/solution.py
@@ -15,7 +15,7 @@
 NEAR = 256
 MEM = 4
 BLK = 128
-AHEAD = 10**10
+AHEAD = 10**9
 ORDER = (3 * 10**8, 3 * 10**8)
 BF = jnp.bfloat16
 F32 = jnp.float32

time: 24 us -> 24 us (level)
  no operation moved by 1% of the time
where the time goes in v6:
time: 24 us; the launch traced here: 23.8 us
  starting transfers between devices  11.9 us (50%)
  Pallas kernels  10 us (42%)
  waiting for transfers between devices  1.05 us (4%)
  between operations  0.82 us (3%)
    ppermute x7, starting transfers between devices, send(): return lax.ppermute(x, ('lat', 'lon'), pairs)  11.9 us
    pallas_call x9, Pallas kernels, call(): pl.pallas_call(kernel, out_shape=out_shape, in_specs=[s for _, s in opera...  10 us
    ppermute x7, waiting for transfers between devices, send(): return lax.ppermute(x, ('lat', 'lon'), pairs)  1.05 us
  transfers between devices with their start and end apart: 7, of which 4 were waited for; matrix products, arithmetic and copies ran while one was open for 0% of the time, Pallas kernels for 24%

profile of v6, /device:TPU:0, one launch (start us, length us, event | category | flops | bytes accessed | tf_op | source)
XLA Modules:
  0.0 23.8 jit_solution(3859704363024356273)
XLA Ops:
  0.6 0.0 copy-start.6
  0.6 0.0 copy-start.2
  0.7 1.2 %shard_map.95 = (bf16[4,8,1024]{2,1,0:T(8,128)(2,1)S(1)}, bf16[4,8,1024]{2,1,0:T(8,128)(2,1)S(1)}, bf16[8,16,640]{2,1,0:T(8,128)(2,1)S(1)}, bf16[8,1536]{1,0:T(8...) custom-call(s32[1]{0:T(128)} %bitcast.row_ref, bf16[4,8,2560]{2,1,0:T(8,128)(2,1)} %field_hbm.1, ...), custom_call_target="tpu_custom_call" | custom-call | flops 1000000000 | bytes 425988 | tf_op jit(solution)/shard_map/pallas_call | solution.py:336
  1.8 0.0 copy-start
  1.8 0.0 copy-start.1
  1.8 0.0 copy-start.3
  1.9 0.0 copy-start.4
  1.9 0.0 copy-start.5
  1.9 0.5 %collective-permute-start = (bf16[4,8,1024]{2,1,0:T(8,128)(2,1)S(1)}, bf16[4,8,1024]{2,1,0:T(8,128)(2,1)S(1)}, u32[]{:S(2)}, u32[]{:S(2)}) collective-permute-start(bf16[4,8,1024]{2,1,0:T(8,128)(2,1)S(1)} %get-tuple-element.24), channel_id=1, source_target_pairs={{0,1},{1,2},{2,3},{3,4},{4,5},{5,6},{6,7},{7,8},{8,9},{9,10},{10,1... | collective-permute-start | bytes 196616 | tf_op jit(solution)/shard_map/ppermute | solution.py:375
  2.4 3.7 %collective-permute-start.1 = (bf16[8,1536]{1,0:T(8,128)(2,1)S(1)}, bf16[8,1536]{1,0:T(8,128)(2,1)S(1)}, u32[]{:S(2)}, u32[]{:S(2)}) collective-permute-start(bf16[8,1536]{1,0:T(8,128)(2,1)S(1)} %get-tuple-element.25), channel_id=1, source_target_pairs={{0,17},{1,18},{2,19},{3,20},{4,21},{5,22},{6,23},{7,24},{8,25},{9,... | collective-permute-start | bytes 73736 | tf_op jit(solution)/shard_map/ppermute | solution.py:375
  6.1 0.5 %collective-permute-start.2 = (bf16[2,16,640]{2,1,0:T(8,128)(2,1)S(1)}, bf16[2,16,640]{2,1,0:T(8,128)(2,1)S(1)}, u32[]{:S(2)}, u32[]{:S(2)}) collective-permute-start(bf16[2,16,640]{2,1,0:T(8,128)(2,1)S(1)} %get-tuple-element.26), channel_id=1, source_target_pairs={{0,16},{1,17},{2,18},{3,19},{4,20},{5,21},{6,22},{7,23},{8,24},{9,... | collective-permute-start | bytes 122888 | tf_op jit(solution)/shard_map/ppermute | solution.py:375
  6.6 2.4 %collective-permute-start.3 = (bf16[4,8,1024]{2,1,0:T(8,128)(2,1)S(1)}, bf16[4,8,1024]{2,1,0:T(8,128)(2,1)S(1)}, u32[]{:S(2)}, u32[]{:S(2)}) collective-permute-start(bf16[4,8,1024]{2,1,0:T(8,128)(2,1)S(1)} %get-tuple-element.27), channel_id=1, source_target_pairs={{0,15},{1,0},{2,1},{3,2},{4,3},{5,4},{6,5},{7,6},{8,7},{9,8},{10,9... | collective-permute-start | bytes 196616 | tf_op jit(solution)/shard_map/ppermute | solution.py:375
  9.1 1.8 %collective-permute-start.4 = (bf16[8,512]{1,0:T(8,128)(2,1)S(1)}, bf16[8,512]{1,0:T(8,128)(2,1)S(1)}, u32[]{:S(2)}, u32[]{:S(2)}) collective-permute-start(bf16[8,512]{1,0:T(8,128)(2,1)S(1)} %get-tuple-element.30), channel_id=1, source_target_pairs={{0,31},{1,16},{2,17},{3,18},{4,19},{5,20},{6,21},{7,22},{8,23},{9,... | collective-permute-start | bytes 24584 | tf_op jit(solution)/shard_map/ppermute | solution.py:375
  10.9 0.2 collective-permute-done.1.rest_1_.dl_ref
  11.1 0.0 collective-permute-done.rest_0_.fl_ref
  11.1 0.0 copy-done.6
  11.1 0.0 collective-permute-done.2.rest_0_.lat_ref
  11.2 0.0 collective-permute-done.3.rest_1_
  11.2 0.0 copy-done.2
  11.2 0.0 copy-done
  11.2 0.0 copy-done.1
  11.2 0.9 %shard_map.98 = (bf16[96,1024]{1,0:T(8,128)(2,1)S(1)}, bf16[96,2560]{1,0:T(8,128)(2,1)S(1)}, bf16[96,1024]{1,0:T(8,128)(2,1)S(1)}) custom-call(s32[1]{0:T(128)} %bitcast.row_ref, s32[2]{0:T(128)S(1)} %copy-done.5, s32[2,2,8]{2,1,0:T(2,128)S(1)} %bitcast.9, s32[2,8]{1,0:T(2,128)S(1)} %copy-done.3, bf16[2,2048,128]{2,1,0:T(8,128)(2,1)S(1)} %copy-done.2, ...), custom_call_target="tpu_custom_call" | custom-call | bytes 3481804 | tf_op jit(solution)/shard_map/pallas_call | solution.py:336
  12.1 0.1 collective-permute-done.4.dr_ref
  12.3 0.9 %shard_map.99 = (bf16[2,16,768]{2,1,0:T(8,128)(2,1)S(1)}, bf16[2,24,640]{2,1,0:T(8,128)(2,1)S(1)}, bf16[96,1024]{1,0:T(8,128)(2,1)S(1)}) custom-call(s32[1]{0:T(128)} %bitcast.row_ref, s32[2]{0:T(128)S(1)} %copy-done.5, s32[2,2,8]{2,1,0:T(2,128)S(1)} %bitcast.10, s32[2,8]{1,0:T(2,128)S(1)} %copy-done.3, bf16[2,2048,128]{2,1,0:T(8,128)(2,1)S(1)} %copy-done.2, ...), custom_call_target="tpu_custom_call" | custom-call | flops 201326592 | bytes 3645644 | tf_op jit(solution)/shard_map/pallas_call | solution.py:336
  13.2 1.4 %collective-permute-start.5 = (bf16[2,16,768]{2,1,0:T(8,128)(2,1)S(1)}, bf16[2,16,768]{2,1,0:T(8,128)(2,1)S(1)}, u32[]{:S(2)}, u32[]{:S(2)}) collective-permute-start(bf16[2,16,768]{2,1,0:T(8,128)(2,1)S(1)} %get-tuple-element.35), channel_id=1, source_target_pairs={{0,16},{1,17},{2,18},{3,19},{4,20},{5,21},{6,22},{7,23},{8,24},{9,... | collective-permute-start | bytes 147464 | tf_op jit(solution)/shard_map/ppermute | solution.py:375
  14.6 2.1 %shard_map.100 = (f32[96,1024]{1,0:T(8,128)S(1)}, bf16[4,24,640]{2,1,0:T(8,128)(2,1)S(1)}, bf16[96,1024]{1,0:T(8,128)(2,1)S(1)}) custom-call(s32[1]{0:T(128)} %bitcast.row_ref, s32[2]{0:T(128)S(1)} %copy-done.5, s32[2,2,8]{2,1,0:T(2,128)S(1)} %bitcast.11, s32[2,8]{1,0:T(2,128)S(1)} %copy-done.3, bf16[2,2048,128]{2,1,0:T(8,128)(2,1)S(1)} %copy-done.2, ...), custom_call_target="tpu_custom_call" | custom-call | flops 402653184 | bytes 3338444 | tf_op jit(solution)/shard_map/pallas_call | solution.py:336
  16.7 0.6 %collective-permute-done.5.got_ref = bf16[2,16,768]{2,1,0:T(8,128)(2,1)S(1)} collective-permute-done((bf16[2,16,768]{2,1,0:T(8,128)(2,1)S(1)}, bf16[2,16,768]{2,1,0:T(8,128)(2,1)S(1)}, u32[]{:S(2)}, u32[]{:S(2)}) %collective-permute-start.5) | collective-permute-done | bytes 49184 | tf_op jit(solution)/shard_map/ppermute | solution.py:375
  17.3 0.7 %shard_map.101 = (bf16[2,16,768]{2,1,0:T(8,128)(2,1)S(1)}, bf16[2,24,640]{2,1,0:T(8,128)(2,1)S(1)}, bf16[96,1024]{1,0:T(8,128)(2,1)S(1)}) custom-call(s32[1]{0:T(128)} %bitcast.row_ref, s32[2]{0:T(128)S(1)} %copy-done.5, s32[2,8]{1,0:T(2,128)S(1)} %copy-done.3, bf16[2,1024,128]{2,1,0:T(8,128)(2,1)S(1)} %copy-done.1, bf16[640,1024]{1,0:T(8,128)(2,1)S(1)} %bitcast.6, ...), custom_call_target="tpu_custom_call" | custom-call | flops 201326592 | bytes 2277452 | tf_op jit(solution)/shard_map/pallas_call | solution.py:336
  18.0 1.4 %collective-permute-start.6 = (bf16[2,16,768]{2,1,0:T(8,128)(2,1)S(1)}, bf16[2,16,768]{2,1,0:T(8,128)(2,1)S(1)}, u32[]{:S(2)}, u32[]{:S(2)}) collective-permute-start(bf16[2,16,768]{2,1,0:T(8,128)(2,1)S(1)} %get-tuple-element.41), channel_id=1, source_target_pairs={{0,16},{1,17},{2,18},{3,19},{4,20},{5,21},{6,22},{7,23},{8,24},{9,... | collective-permute-start | bytes 147464 | tf_op jit(solution)/shard_map/ppermute | solution.py:375
  19.5 2.6 %shard_map.102 = (f32[64,1024]{1,0:T(8,128)S(1)}, bf16[4,16,640]{2,1,0:T(8,128)(2,1)S(1)}, bf16[2,16,4,1024]{3,2,1,0:T(4,128)(2,1)}) custom-call(s32[1]{0:T(128)} %bitcast.row_ref, s32[2]{0:T(128)S(1)} %copy-done.5, s32[2,2,8]{2,1,0:T(2,128)S(1)} %bitcast.12, s32[2,8]{1,0:T(2,128)S(1)} %copy-done.3, bf16[2,2048,128]{2,1,0:T(8,128)(2,1)S(1)} %copy-done.2, ...), custom_call_target="tpu_custom_call" | custom-call | flops 402653184 | bytes 3461324 | tf_op jit(solution)/shard_map/pallas_call | solution.py:336
  22.1 0.1 collective-permute-done.6.got_ref
  22.2 1.6 %shard_map.103 = (bf16[4,8,2560]{2,1,0:T(8,128)(2,1)}, bf16[2,16,4,1024]{3,2,1,0:T(4,128)(2,1)}) custom-call(s32[1]{0:T(128)} %bitcast.row_ref, s32[2]{0:T(128)S(1)} %copy-done.5, s32[2,8]{1,0:T(2,128)S(1)} %copy-done.3, bf16[2,1024,128]{2,1,0:T(8,128)(2,1)S(1)} %copy-done.1, bf16[640,1024]{1,0:T(8,128)(2,1)S(1)} %bitcast.8, ...), custom_call_target="tpu_custom_call", output_to_operand_aliasing={{1}: (8, {})} | custom-call | flops 201326592 | bytes 2490444 | tf_op jit(solution)/shard_map/pallas_call | solution.py:336
  (5 shorter events, 0.1 us)
Async XLA Ops:
  0.6 10.4 %copy-start.6 = (bf16[2,16,4,1024]{3,2,1,0:T(4,128)(2,1)S(1)}, bf16[2,16,4,1024]{3,2,1,0:T(4,128)(2,1)}, u32[]{:S(2)}) copy-start(bf16[2,16,4,1024]{3,2,1,0:T(4,128)(2,1)} %state_ref.3) | copy-start | bytes 786436
  0.6 10.5 %copy-start.2 = (bf16[2,2048,128]{2,1,0:T(8,128)(2,1)S(1)}, bf16[2,2048,128]{2,1,0:T(8,128)(2,1)}, u32[]{:S(2)}) copy-start(bf16[2,2048,128]{2,1,0:T(8,128)(2,1)} %coup_ref.7) | copy-start | bytes 3145732
  1.8 9.4 %copy-start = (bf16[1,640,1024]{2,1,0:T(8,128)(2,1)S(1)}, bf16[1,640,1024]{2,1,0:T(8,128)(2,1)}, u32[]{:S(2)}) copy-start(bf16[1,640,1024]{2,1,0:T(8,128)(2,1)} %param.14) | copy-start | bytes 3932164
  1.8 9.4 %copy-start.1 = (bf16[2,1024,128]{2,1,0:T(8,128)(2,1)S(1)}, bf16[2,1024,128]{2,1,0:T(8,128)(2,1)}, u32[]{:S(2)}) copy-start(bf16[2,1024,128]{2,1,0:T(8,128)(2,1)} %inp_ref.11) | copy-start | bytes 1572868
  1.8 9.4 %copy-start.3 = (s32[2,8]{1,0:T(2,128)S(1)}, s32[2,8]{1,0:T(2,128)}, u32[]{:S(2)}) copy-start(s32[2,8]{1,0:T(2,128)} %iidx_ref.11) | copy-start | bytes 196
  1.9 9.4 %copy-start.4 = (s32[2,8,2]{1,2,0:T(2,128)S(1)}, s32[2,8,2]{1,2,0:T(2,128)}, u32[]{:S(2)}) copy-start(s32[2,8,2]{1,2,0:T(2,128)} %param.11) | copy-start | bytes 388
  1.9 9.4 %copy-start.5 = (s32[2]{0:T(128)S(1)}, s32[2]{0:T(128)}, u32[]{:S(2)}) copy-start(s32[2]{0:T(128)} %band_ref.11) | copy-start | bytes 28
  1.9 9.2 %collective-permute-start = (bf16[4,8,1024]{2,1,0:T(8,128)(2,1)S(1)}, bf16[4,8,1024]{2,1,0:T(8,128)(2,1)S(1)}, u32[]{:S(2)}, u32[]{:S(2)}) collective-permute-start(bf16[4,8,1024]{2,1,0:T(8,128)(2,1)S(1)} %get-tuple-element.24), channel_id=1, source_target_pairs={{0,1},{1,2},{2,3},{3,4},{4,5},{5,6},{6,7},{7,8},{8,9},{9,10},{10,1... | collective-permute-start | bytes 196616 | tf_op jit(solution)/shard_map/ppermute | solution.py:375
  2.4 8.7 %collective-permute-start.1 = (bf16[8,1536]{1,0:T(8,128)(2,1)S(1)}, bf16[8,1536]{1,0:T(8,128)(2,1)S(1)}, u32[]{:S(2)}, u32[]{:S(2)}) collective-permute-start(bf16[8,1536]{1,0:T(8,128)(2,1)S(1)} %get-tuple-element.25), channel_id=1, source_target_pairs={{0,17},{1,18},{2,19},{3,20},{4,21},{5,22},{6,23},{7,24},{8,25},{9,... | collective-permute-start | bytes 73736 | tf_op jit(solution)/shard_map/ppermute | solution.py:375
  6.1 5.0 %collective-permute-start.2 = (bf16[2,16,640]{2,1,0:T(8,128)(2,1)S(1)}, bf16[2,16,640]{2,1,0:T(8,128)(2,1)S(1)}, u32[]{:S(2)}, u32[]{:S(2)}) collective-permute-start(bf16[2,16,640]{2,1,0:T(8,128)(2,1)S(1)} %get-tuple-element.26), channel_id=1, source_target_pairs={{0,16},{1,17},{2,18},{3,19},{4,20},{5,21},{6,22},{7,23},{8,24},{9,... | collective-permute-start | bytes 122888 | tf_op jit(solution)/shard_map/ppermute | solution.py:375
  6.6 4.5 %collective-permute-start.3 = (bf16[4,8,1024]{2,1,0:T(8,128)(2,1)S(1)}, bf16[4,8,1024]{2,1,0:T(8,128)(2,1)S(1)}, u32[]{:S(2)}, u32[]{:S(2)}) collective-permute-start(bf16[4,8,1024]{2,1,0:T(8,128)(2,1)S(1)} %get-tuple-element.27), channel_id=1, source_target_pairs={{0,15},{1,0},{2,1},{3,2},{4,3},{5,4},{6,5},{7,6},{8,7},{9,8},{10,9... | collective-permute-start | bytes 196616 | tf_op jit(solution)/shard_map/ppermute | solution.py:375
  9.1 3.2 %collective-permute-start.4 = (bf16[8,512]{1,0:T(8,128)(2,1)S(1)}, bf16[8,512]{1,0:T(8,128)(2,1)S(1)}, u32[]{:S(2)}, u32[]{:S(2)}) collective-permute-start(bf16[8,512]{1,0:T(8,128)(2,1)S(1)} %get-tuple-element.30), channel_id=1, source_target_pairs={{0,31},{1,16},{2,17},{3,18},{4,19},{5,20},{6,21},{7,22},{8,23},{9,... | collective-permute-start | bytes 24584 | tf_op jit(solution)/shard_map/ppermute | solution.py:375
  13.2 4.2 %collective-permute-start.5 = (bf16[2,16,768]{2,1,0:T(8,128)(2,1)S(1)}, bf16[2,16,768]{2,1,0:T(8,128)(2,1)S(1)}, u32[]{:S(2)}, u32[]{:S(2)}) collective-permute-start(bf16[2,16,768]{2,1,0:T(8,128)(2,1)S(1)} %get-tuple-element.35), channel_id=1, source_target_pairs={{0,16},{1,17},{2,18},{3,19},{4,20},{5,21},{6,22},{7,23},{8,24},{9,... | collective-permute-start | bytes 147464 | tf_op jit(solution)/shard_map/ppermute | solution.py:375
  18.0 4.2 %collective-permute-start.6 = (bf16[2,16,768]{2,1,0:T(8,128)(2,1)S(1)}, bf16[2,16,768]{2,1,0:T(8,128)(2,1)S(1)}, u32[]{:S(2)}, u32[]{:S(2)}) collective-permute-start(bf16[2,16,768]{2,1,0:T(8,128)(2,1)S(1)} %get-tuple-element.41), channel_id=1, source_target_pairs={{0,16},{1,17},{2,18},{3,19},{4,20},{5,21},{6,22},{7,23},{8,24},{9,... | collective-permute-start | bytes 147464 | tf_op jit(solution)/shard_map/ppermute | solution.py:375
